TPU v7x, 32 devices: a whole 2x2x4 slice. The times are simulated.
32 devices in a mesh: ha: 8 (over y, x, core), wa: 4 (over z).
Axes of the slice: x: 2, y: 2, z: 4, core: 2. Of those that a mesh axis runs over, the one named last changes fastest.
Arguments:
- block_input: bfloat16 [16, 64, 128, 128], P(None, 'ha', 'wa'), may hold values from -18 to 18
- timesteps: int32 [16], replicated, may hold values from 0 to 999
- aug_levels: int32 [16], replicated, may hold values from 0 to 999
- text_pooled: bfloat16 [16, 4096], replicated, may hold values from -6 to 6
- gain_one: bfloat16 [128], replicated, may hold values from 0.25 to 1.75
- bias_one: bfloat16 [128], replicated, may hold values from -3 to 3
- conv_one: bfloat16 [3, 3, 128, 128], replicated, may hold values from -0.1875 to 0.1875
- conv_one_bias: bfloat16 [128], replicated, may hold values from -3 to 3
- gain_two: bfloat16 [128], replicated, may hold values from 0.25 to 1.75
- bias_two: bfloat16 [128], replicated, may hold values from -3 to 3
- film_weight: bfloat16 [4608, 256], replicated, may hold values from -0.125 to 0.125
- film_bias: bfloat16 [256], replicated, may hold values from -2 to 2
- conv_two: bfloat16 [3, 3, 128, 128], replicated, may hold values from -0.1875 to 0.1875
- conv_two_bias: bfloat16 [128], replicated, may hold values from -3 to 3
- cotangent: bfloat16 [16, 64, 128, 128], P(None, 'ha', 'wa'), may hold values from -6 to 6
Outputs:
- mixed: bfloat16 [16, 64, 128, 128], P(None, 'ha', 'wa')
- input_grad: bfloat16 [16, 64, 128, 128], P(None, 'ha', 'wa')
- text_grad: float32 [16, 4096], replicated
- gain_one_grad: float32 [128], replicated
- bias_one_grad: float32 [128], replicated
- conv_one_grad: float32 [3, 3, 128, 128], replicated
- conv_one_bias_grad: float32 [128], replicated
- gain_two_grad: float32 [128], replicated
- bias_two_grad: float32 [128], replicated
- film_weight_grad: float32 [4608, 256], replicated
- film_bias_grad: float32 [256], replicated
- conv_two_grad: float32 [3, 3, 128, 128], replicated
- conv_two_bias_grad: float32 [128], replicated
All inputs are finite; a program needn't handle non-finite values.
Results may differ from a plain program's by a relative error of at most 0.0051.
Values may be sent and summed in bfloat16 or wider, within the bound.
No kernel may reach another device: no remote copies, remote signals or barrier semaphores. Data moves between devices by JAX's collectives and lax.ppermute only.
A program may use at most 128 MiB of HBM per device.

v0:
```python
import functools
import math

import jax
import jax.numpy as jnp
import numpy as np
from jax import lax
from jax.experimental import pallas as pl
from jax.experimental.pallas import tpu as pltpu
from jax.sharding import PartitionSpec as P

GROUPS = 32
TEMB = 256
EPSILON = 1e-05
INV_ROOT = 1.0 / math.sqrt(2.0)
AXES = ("ha", "wa")
F32 = jnp.float32
BF16 = jnp.bfloat16
NEAR = pl.BlockSpec(memory_space=pltpu.VMEM)
FAR = pl.BlockSpec(memory_space=pl.ANY)
MIB = 1 << 20


def shaped(shape, dtype):
    return jax.ShapeDtypeStruct(shape, dtype)


def kernel_call(
    body, far=(), near=(), tiny=(), far_out=(), near_out=(), tiny_out=(), scratch=(), sems=0, cost=1.0,
    after=(), after_near=(), scalars=(), limit=48,
):
    pinned = lambda arrays: [pltpu.with_memory_space_constraint(array, pltpu.HBM) for array in arrays]
    given = len(far) + len(near)
    held = len(after) + len(after_near)
    copies = len(tiny) + len(tiny_out)

    def run(*refs):
        refs = list(refs)
        take = lambda count: [refs.pop(0) for _ in range(count)]
        inputs = take(given)
        tiny_far = take(len(tiny))
        scalar_refs = take(len(scalars))
        take(held)
        outputs = take(len(far_out) + len(near_out))
        tiny_out_far = take(len(tiny_out))
        tiny_refs = take(len(tiny))
        tiny_out_refs = take(len(tiny_out))
        mover = None
        if sems + copies:
            mover = Mover(refs.pop(), [(f, n) for f, n in zip(tiny_far, tiny_refs)])
        body(*inputs, *tiny_refs, *scalar_refs, *outputs, *tiny_out_refs, *refs, *([mover] if mover else []))
        if mover:
            for source, target in zip(tiny_out_refs, tiny_out_far):
                mover.put(source, target)
            mover.finish()

    return pl.pallas_call(
        run,
        out_shape=(
            *(pltpu.HBM(out.shape, out.dtype) for out in far_out),
            *near_out,
            *(pltpu.HBM(out.shape, out.dtype) for out in tiny_out),
        ),
        in_specs=[FAR] * len(far)
        + [NEAR] * len(near)
        + [FAR] * len(tiny)
        + [pl.BlockSpec(memory_space=pltpu.SMEM)] * len(scalars)
        + [FAR] * held,
        out_specs=(FAR,) * len(far_out) + (NEAR,) * len(near_out) + (FAR,) * len(tiny_out),
        scratch_shapes=buffers(*tiny, *tiny_out)
        + tuple(scratch)
        + ((pltpu.SemaphoreType.DMA((sems + copies,)),) if sems + copies else ()),
        compiler_params=pltpu.CompilerParams(vmem_limit_bytes=limit * MIB),
        name=getattr(body, "func", body).__name__,
        cost_estimate=pl.CostEstimate(flops=int(cost * 1.1e9), bytes_accessed=0, transcendentals=0),
    )(*pinned(far), *near, *pinned(tiny), *scalars, *pinned(after), *after_near)


def buffers(*arrays):
    return tuple(pltpu.VMEM(a.shape, a.dtype) for a in arrays)


class Mover:
    def __init__(self, sems, first):
        self.sems = sems
        self.used = 0
        self.open = []
        self.first = [self.start(source, target) for source, target in first]

    def start(self, source, target):
        copy = pltpu.make_async_copy(source, target, self.sems.at[self.used])
        self.used += 1
        copy.start()
        return copy

    def ready(self):
        for copy in self.first:
            copy.wait()

    def put(self, source, target):
        self.open.append(self.start(source, target))

    def finish(self):
        for copy in self.open:
            copy.wait()


def pieces(count, size):
    return [(at, min(at + size, count)) for at in range(0, count, size)]


def lanes_of(shape):
    return lax.broadcasted_iota(jnp.int32, shape, 1)


def group_total(values):
    chans = values.shape[1]
    lane = lanes_of(values.shape)
    step = 1
    while step < chans // GROUPS:
        up = pltpu.roll(values, chans - step, 1)
        down = pltpu.roll(values, step, 1)
        values = values + jnp.where((lane & step) == 0, up, down)
        step *= 2
    return values


def pack_pair(first, second):
    half = first.shape[0] // 2
    lane = lanes_of((half, first.shape[1])) & 3
    return jnp.where(
        lane == 0,
        first[:half],
        jnp.where(lane == 1, second[:half], jnp.where(lane == 2, first[half:], second[half:])),
    )


def unpack_at(packed, place):
    lane = lanes_of(packed.shape) & 3
    top = group_total(jnp.where(lane == place, packed, 0.0))
    low = group_total(jnp.where(lane == place + 2, packed, 0.0))
    return jnp.concatenate([top, low], axis=0)


def merge_moments(gathered_ref, local_count):
    parts = gathered_ref.shape[0]
    chans = gathered_ref.shape[2]
    every = gathered_ref[...]
    total = jnp.sum(every, axis=0)
    mean = total * (1.0 / parts)
    apart = every - mean[None]
    between = jnp.sum(apart * apart, axis=0)
    square = pltpu.roll(total, chans - 1, 1) + local_count * between
    inv = lax.rsqrt(square * (1.0 / (local_count * parts)) + EPSILON)
    return unpack_at(mean, 0), unpack_at(inv, 0)


def local_moments(total, square, pilot, pixels, per):
    off = total * (1.0 / pixels)
    mean = pilot + off
    apart = square - total * off
    group_mean = group_total(mean) * (1.0 / per)
    shift = mean - group_mean
    return group_mean, group_total(apart + pixels * shift * shift)


def sigmoid(values):
    return 0.5 + 0.5 * jnp.tanh(0.5 * values)


def forward_weights(kernel_ref, pair_ref):
    chans = kernel_ref.shape[2]
    zero = jnp.zeros((chans, chans), BF16)
    for row in range(3):
        for col in range(4):
            at = (row * 4 + col) * chans
            pair_ref[at : at + chans, 0:chans] = kernel_ref[row, col] if col < 3 else zero
            pair_ref[at : at + chans, chans:] = kernel_ref[row, col - 1] if col > 0 else zero


def backward_weights(kernel_ref, pair_ref):
    chans = kernel_ref.shape[2]
    zero = jnp.zeros((chans, chans), BF16)
    for row in range(3):
        for col in range(4):
            at = (row * 4 + col) * chans
            pair_ref[0:chans, at : at + chans] = kernel_ref[2 - row, 2 - col] if col < 3 else zero
            pair_ref[chans:, at : at + chans] = kernel_ref[2 - row, 3 - col] if col > 0 else zero


def convolve(cells_ref, pair_ref, transposed, rows, first, last, take):
    images, chans = cells_ref.shape[2:]
    pairs = (last - first) // 2
    parts = []
    for row in range(3):
        for col in range(4):
            window = [cells_ref[first + 2 * q + col, row : row + rows] for q in range(pairs)]
            parts.append(jnp.stack(window).reshape(pairs * rows * images, chans))
    wide = jnp.concatenate(parts, axis=1)
    contract = ((1,), (1,)) if transposed else ((1,), (0,))
    made = lax.dot_general(wide, pair_ref[...], (contract, ((), ())), preferred_element_type=F32)
    made = made.reshape(pairs, rows, images, 2 * chans)
    for q in range(pairs):
        for side in range(2):
            take(first + 2 * q + side, made[q, :, :, side * chans : (side + 1) * chans])


def grad_terms(cells_ref, grads_ref):
    cols, rows, images, chans = grads_ref.shape
    pixels = cols * rows * images
    windows = [
        cells_ref[col : col + cols, row : row + rows].reshape(pixels, chans) for row in range(3) for col in range(3)
    ]
    return lax.dot_general(
        grads_ref[...].reshape(pixels, chans),
        jnp.concatenate(windows, axis=1),
        (((0,), (0,)), ((), ())),
        preferred_element_type=F32,
    )


def split_taps(every, keep_ref, send_ref):
    chans = every.shape[0]
    half = chans // 2
    first = lax.axis_index("ha") % 2 == 0
    for tap in range(9):
        made = every[:, tap * chans : (tap + 1) * chans].T
        at = tap * half
        keep_ref[at : at + half, :] = jnp.where(first, made[:half], made[half:])
        send_ref[at : at + half, :] = jnp.where(first, made[half:], made[:half])


def at_edges():
    tall = lax.axis_index("ha")
    wide = lax.axis_index("wa")
    return (
        tall == 0,
        tall == lax.axis_size("ha") - 1,
        wide == 0,
        wide == lax.axis_size("wa") - 1,
    )


def clear_border(cells_ref, width, first=0, last=None):
    top, bottom, left, right = at_edges()
    cols, rows, images, chans = cells_ref.shape
    last = cols if last is None else last
    dtype = cells_ref.dtype

    @pl.when(top)
    def _():
        cells_ref[first:last, 0:width] = jnp.zeros((last - first, width, images, chans), dtype)

    @pl.when(bottom)
    def _():
        cells_ref[first:last, rows - width :] = jnp.zeros((last - first, width, images, chans), dtype)

    if first == 0:

        @pl.when(left)
        def _():
            cells_ref[0:width] = jnp.zeros((width, rows, images, chans), dtype)

    if last == cols:

        @pl.when(right)
        def _():
            cells_ref[cols - width :] = jnp.zeros((width, rows, images, chans), dtype)


def send_payload(mover, packed, pay_ref, stage_ref):
    stage_ref[...] = jnp.broadcast_to(packed[None], stage_ref.shape)
    mover.put(stage_ref, pay_ref)


def prepare_x(x_far, xt_far, near_ref, next_ref, sides_ref, moments_ref, x_ref, xt_ref, mover):
    images, rows, cols, chans = x_ref.shape
    steps = pieces(rows, 2)
    loads = [mover.start(x_far.at[:, a:b], x_ref.at[:, a:b]) for a, b in steps]
    total = jnp.zeros((images, chans), F32)
    square = total
    for (a, b), load in zip(steps, loads):
        load.wait()
        if a == 0:
            pilot = x_ref[:, 0, 0].astype(F32)
        for row in range(a, b):
            x = jnp.swapaxes(x_ref[:, row].astype(F32), 0, 1)
            xt_ref[:, row] = x.astype(BF16)
            apart = x - pilot[None]
            total = total + jnp.sum(apart, axis=0)
            square = square + jnp.sum(apart * apart, axis=0)
        mover.put(xt_ref.at[:, a:b], xt_far.at[:, a:b])
    mean, spread = local_moments(total, square, pilot, rows * cols, chans // GROUPS)
    moments_ref[...] = pack_pair(mean, spread)
    outer(xt_ref, near_ref, next_ref, sides_ref)


def is_even(axis="ha"):
    return lax.axis_index(axis) % 2 == 0


def outer(cells, near_ref, next_ref, sides_ref):
    cols, rows = cells.shape[0:2]
    down, up = cells[:, rows - 2 :], cells[:, 0:2]
    near_ref[...] = jnp.where(is_even(), down, up)
    next_ref[...] = jnp.where(is_even(), up, down)
    sides_ref[0:2] = cells[0:2]
    sides_ref[2:4] = cells[cols - 2 :]


def prepare_g(
    c_far, moments_ref, gt_far, pay_far, near_ref, next_ref, sides_ref, bias_ref, c_ref, gt_ref, stage_ref, mover
):
    images, rows, cols, chans = c_ref.shape
    steps = pieces(rows, 2)
    loads = [mover.start(c_far.at[:, a:b], c_ref.at[:, a:b]) for a, b in steps]
    send_payload(mover, moments_ref[...], pay_far, stage_ref)
    bias = jnp.zeros((images, chans), F32)
    for (a, b), load in zip(steps, loads):
        load.wait()
        for row in range(a, b):
            grad = jnp.swapaxes(c_ref[:, row].astype(F32) * INV_ROOT, 0, 1).astype(BF16)
            gt_ref[:, row] = grad
            bias = bias + jnp.sum(grad.astype(F32), axis=0)
        mover.put(gt_ref.at[:, a:b], gt_far.at[:, a:b])
    bias_ref[...] = bias
    outer(gt_ref, near_ref, next_ref, sides_ref)


def edge_columns(sides_ref, near_ref, next_ref, one_ref, other_ref):
    cols, rows = near_ref.shape[0], sides_ref.shape[1]
    even = is_even("wa")

    def piece(left, right):
        return jnp.where(even, right, left), jnp.where(even, left, right)

    near = piece(near_ref[0:2], near_ref[cols - 2 : cols])
    following = piece(next_ref[0:2], next_ref[cols - 2 : cols])
    own = piece(sides_ref[0:2], sides_ref[2:4])
    for at, ref in enumerate((one_ref, other_ref)):
        ref[:, 0:2] = jnp.where(is_even(), following[at], near[at])
        ref[:, 2 : rows + 2] = own[at]
        ref[:, rows + 2 :] = jnp.where(is_even(), near[at], following[at])


def fill_halo(cells_ref, near_ref, next_ref, one_ref, other_ref, change):
    cols, rows = near_ref.shape[0], cells_ref.shape[1] - 4

    def halo_column(col, _):
        near, next_ = near_ref[pl.ds(col, 1)], next_ref[pl.ds(col, 1)]
        cells_ref[pl.ds(col + 2, 1), 0:2] = change(jnp.where(is_even(), next_, near))
        cells_ref[pl.ds(col + 2, 1), rows + 2 :] = change(jnp.where(is_even(), near, next_))
        return 0

    even = is_even("wa")
    cells_ref[0:2] = change(jnp.where(even, other_ref[...], one_ref[...]))
    cells_ref[cols + 2 :] = change(jnp.where(even, one_ref[...], other_ref[...]))
    lax.fori_loop(0, cols, halo_column, 0, unroll=4)


def first_half(
    xt_far, kernel_far, near_ref, next_ref, one_ref, other_ref, gathered_ref, gain_ref, bias_ref, kbias_ref,
    act_far, mid_far, pay_far, stat_ref,
    xt_ref, kernel_ref, act_ref, mid_ref, stage_ref, pair_ref, mover,
):
    cols, rows, images, chans = xt_ref.shape
    per = chans // GROUPS
    load = mover.start(kernel_far, kernel_ref)
    steps = pieces(cols, 8)
    own = [mover.start(xt_far.at[a:b], xt_ref.at[a:b]) for a, b in steps]
    mean, inv = merge_moments(gathered_ref, rows * cols * per)
    stat_ref[0] = mean
    stat_ref[1] = inv
    mover.ready()
    slope = 0.5 * inv * gain_ref[...].astype(F32)
    offset = 0.5 * bias_ref[...].astype(F32)

    def act(cells):
        value = (cells.astype(F32) - mean) * slope + offset
        return (value + value * jnp.tanh(value)).astype(BF16)

    def column(col, _):
        act_ref[pl.ds(col + 2, 1), 2 : rows + 2] = act(xt_ref[pl.ds(col, 1)])
        return 0

    fill_halo(act_ref, near_ref, next_ref, one_ref, other_ref, act)
    for (a, b), copy in zip(steps, own):
        copy.wait()
        lax.fori_loop(a, b, column, 0, unroll=2)
    clear_border(act_ref, 2)
    load.wait()
    forward_weights(kernel_ref, pair_ref)
    mover.put(act_ref, act_far)

    wide = cols + 2
    kbias = kbias_ref[...].astype(F32)
    state = [None, jnp.zeros((images, chans), F32), jnp.zeros((images, chans), F32)]

    def take(col, values):
        values = values + kbias
        mid_ref[col] = values
        if 1 <= col <= cols:
            own = values[1 : rows + 1]
            if state[0] is None:
                state[0] = own[0]
            apart = own - state[0][None]
            state[1] = state[1] + jnp.sum(apart, axis=0)
            state[2] = state[2] + jnp.sum(apart * apart, axis=0)

    for a, b in pieces(wide, 10):
        convolve(act_ref, pair_ref, False, rows + 2, a, b, take)
        mover.put(mid_ref.at[a:b], mid_far.at[a:b])
    pilot, total, square = state
    mean, spread = local_moments(total, square, pilot, rows * cols, per)
    send_payload(mover, pack_pair(mean, spread), pay_far, stage_ref)


def back_two(
    gt_far, kernel_far, weight_far, near_ref, next_ref, one_ref, other_ref, *refs,
):
    text_ref, fbias_ref, freqs_ref, times_ref, levels_ref, out_far, film_ref, ints_ref, *refs = refs
    gt_ref, kernel_ref, weight_ref, cells_ref, out_ref, pair_ref, mover = refs
    cols, rows = gt_ref.shape[0:2]
    load = mover.start(kernel_far, kernel_ref)
    steps = pieces(cols, 8)
    own = [mover.start(gt_far.at[a:b], gt_ref.at[a:b]) for a, b in steps]
    late = mover.start(weight_far, weight_ref)
    fill_halo(cells_ref, near_ref, next_ref, one_ref, other_ref, lambda cells: cells)
    load.wait()
    backward_weights(kernel_ref, pair_ref)
    mover.ready()
    text = text_ref[...].astype(F32)
    half = TEMB // 2
    for at, source_ref in ((0, times_ref), (TEMB, levels_ref)):
        angles = [source_ref[image].astype(F32) * freqs_ref[...] for image in range(text_ref.shape[0])]
        angles = jnp.concatenate(angles, axis=0)
        for start, embed in ((at, jnp.sin(angles)), (at + half, jnp.cos(angles))):
            ints_ref[:, start : start + half] = (embed * sigmoid(embed)).astype(BF16)
    act = jnp.concatenate([ints_ref[...], (text * sigmoid(text)).astype(BF16)], axis=1)
    for (a, b), copy in zip(steps, own):
        copy.wait()
        cells_ref[a + 2 : b + 2, 2 : rows + 2] = gt_ref[a:b]
    clear_border(cells_ref, 2)
    for a, b in pieces(cols + 2, 10):
        convolve(cells_ref, pair_ref, True, rows + 2, a, b, lambda col, values: out_ref.__setitem__(col, values))
        mover.put(out_ref.at[a:b], out_far.at[a:b])
    late.wait()
    film_ref[...] = jnp.dot(act, weight_ref[...], preferred_element_type=F32) + fbias_ref[...].astype(F32)


def second_values(stat, gain_ref, bias_ref, film_ref):
    mean, inv = stat
    chans = mean.shape[1]
    scale = 1.0 + film_ref[:, 0:chans]
    slope = gain_ref[...].astype(F32) * scale
    half_slope = 0.5 * slope
    half_offset = 0.5 * (bias_ref[...].astype(F32) * scale + film_ref[:, chans:])

    def values(mid, back):
        hat = (mid - mean) * inv
        pre = hat * half_slope + half_offset
        bend = jnp.tanh(pre)
        more = 1.0 + bend
        grad = back * (0.5 * more * (1.0 + pre * (1.0 - bend)))
        return hat, pre * more, grad

    return slope, values


def second_norm(
    mid_far, back_far, gathered_ref, gain_ref, bias_ref, film_ref,
    act_far, pre_far, pay_far, sums_ref, stat_ref,
    mid_ref, back_ref, act_ref, pre_ref, stage_ref, mover,
):
    wide, tall, images, chans = mid_ref.shape
    cols, rows = wide - 2, tall - 2
    per = chans // GROUPS
    steps = pieces(wide, 9)
    loads = []
    for a, b in steps:
        loads.append(
            [mover.start(f.at[a:b], n.at[a:b]) for f, n in ((mid_far, mid_ref), (back_far, back_ref))]
        )
    mean, inv = merge_moments(gathered_ref, rows * cols * per)
    stat_ref[0] = mean
    stat_ref[1] = inv
    mover.ready()
    slope, values = second_values((mean, inv), gain_ref, bias_ref, film_ref)

    def column(col, inner):
        hat, act, grad = values(mid_ref[col], back_ref[col])
        act_ref[col] = act.astype(BF16)
        pre_ref[col] = grad.astype(BF16)
        if inner is None:
            return None
        own = grad[1 : rows + 1]
        plain, cross = inner
        return plain + jnp.sum(own, axis=0), cross + jnp.sum(own * hat[1 : rows + 1], axis=0)

    zero = jnp.zeros((images, chans), F32)
    inner = (zero, zero)
    for (a, b), pair in zip(steps, loads):
        for load in pair:
            load.wait()
        if a == 0:
            column(0, None)
        inner = lax.fori_loop(max(a, 1), min(b, cols + 1), column, inner)
        if b == wide:
            column(wide - 1, None)
        clear_border(act_ref, 1, a, b)
        mover.put(act_ref.at[a:b], act_far.at[a:b])
        mover.put(pre_ref.at[a:b], pre_far.at[a:b])
    plain, cross = inner
    sums_ref[0] = plain
    sums_ref[1] = cross
    send_payload(mover, pack_pair(group_total(plain * slope), group_total(cross * slope)), pay_far, stage_ref)


def kernel_two(
    act_far, gt_far, sums_ref, bias_ref, keep_far, send_far, act_ref, gt_ref, keep_ref, send_ref, mover
):
    for load in [mover.start(act_far, act_ref), mover.start(gt_far, gt_ref)]:
        load.wait()
    split_taps(grad_terms(act_ref, gt_ref), keep_ref, send_ref)
    mover.ready()
    images, chans = bias_ref.shape
    at = 9 * (chans // 2)
    total = jnp.sum(bias_ref[...], axis=0, keepdims=True)
    for ref in (keep_ref, send_ref):
        ref[at : at + images] = sums_ref[0]
        ref[at + images : at + 2 * images] = sums_ref[1]
        ref[at + 2 * images :] = jnp.broadcast_to(total, (ref.shape[0] - at - 2 * images, chans))
    mover.put(keep_ref, keep_far)
    mover.put(send_ref, send_far)


def mix(
    act_far, kernel_far, xt_far, kbias_ref, out_far, act_ref, kernel_ref, xt_ref, branch_ref, out_ref, pair_ref, mover
):
    images, rows, cols, chans = out_ref.shape
    loads = [mover.start(f, n) for f, n in ((kernel_far, kernel_ref), (act_far, act_ref), (xt_far, xt_ref))]
    loads[0].wait()
    forward_weights(kernel_ref, pair_ref)
    mover.ready()
    kbias = kbias_ref[...].astype(F32)
    loads[1].wait()
    convolve(
        act_ref, pair_ref, False, rows, 0, cols, lambda col, values: branch_ref.__setitem__(col, values + kbias)
    )
    loads[2].wait()
    for a, b in pieces(rows, 2):
        for row in range(a, b):
            mixed = jnp.swapaxes((xt_ref[:, row].astype(F32) + branch_ref[:, row]) * INV_ROOT, 0, 1)
            out_ref[:, row] = mixed.astype(BF16)
        mover.put(out_ref.at[:, a:b], out_far.at[:, a:b])


def middle_grad(
    mid_far, pre_far, act_far, keep_two_far, gathered_ref, stat_ref, gain_ref, film_ref,
    low_far, keep_ref, send_ref, two_ref,
    mid_ref, pre_ref, act_ref, low_ref, mover,
):
    wide, tall, images, chans = mid_ref.shape
    cols, rows = wide - 2, tall - 2
    steps = pieces(wide, 9)
    loads = []
    for a, b in steps:
        loads.append([mover.start(f.at[a:b], n.at[a:b]) for f, n in ((mid_far, mid_ref), (pre_far, pre_ref))])
    late = [mover.start(f, n) for f, n in ((act_far, act_ref), (keep_two_far, two_ref))]
    count = lax.axis_size("ha") * lax.axis_size("wa") * rows * cols * (chans // GROUPS)
    packed = jnp.sum(gathered_ref[...], axis=0) * (1.0 / count)
    mover.ready()
    mean = stat_ref[0]
    inv = stat_ref[1]
    plain = unpack_at(packed, 0) * inv
    cross = unpack_at(packed, 1) * inv * inv
    slope = gain_ref[...].astype(F32) * (1.0 + film_ref[:, 0:chans]) * inv

    def low_column(col, total):
        low = (pre_ref[col].astype(F32) * slope - plain - (mid_ref[col] - mean) * cross).astype(BF16)
        low_ref[col] = low
        if total is None:
            return None
        return total + jnp.sum(low[1 : rows + 1].astype(F32), axis=0)

    kbias = jnp.zeros((images, chans), F32)
    for (a, b), pair in zip(steps, loads):
        for load in pair:
            load.wait()
        if a == 0:
            low_column(0, None)
        kbias = lax.fori_loop(max(a, 1), min(b, cols + 1), low_column, kbias)
        if b == wide:
            low_column(wide - 1, None)
        clear_border(low_ref, 1, a, b)
        mover.put(low_ref.at[a:b], low_far.at[a:b])
    for load in late:
        load.wait()
    own = low_ref.at[1 : wide - 1, 1 : tall - 1]
    split_taps(grad_terms(act_ref.at[1 : wide + 1, 1 : tall + 1], own), keep_ref, send_ref)
    at = 9 * (chans // 2)
    for ref in (keep_ref, send_ref):
        ref[at:] = jnp.broadcast_to(jnp.sum(kbias, axis=0, keepdims=True), (ref.shape[0] - at, chans))


def back_one(
    low_far, xt_far, kernel_far, stat_ref, gain_ref, bias_ref, grad_far, pay_ref, low_ref, xt_ref, kernel_ref, out_ref, pair_ref, mover
):
    cols, rows, images, chans = xt_ref.shape
    loads = [mover.start(f, n) for f, n in ((kernel_far, kernel_ref), (low_far, low_ref), (xt_far, xt_ref))]
    loads[0].wait()
    backward_weights(kernel_ref, pair_ref)
    loads[1].wait()
    loads[2].wait()
    mover.ready()
    mean = stat_ref[0]
    inv = stat_ref[1]
    gain = gain_ref[...].astype(F32)
    bias = bias_ref[...].astype(F32)
    state = [jnp.zeros((images, chans), F32), jnp.zeros((images, chans), F32)]

    def take(col, values):
        hat = (xt_ref[col].astype(F32) - mean) * inv
        norm = hat * gain + bias
        sigma = sigmoid(norm)
        grad = values * (sigma * (1.0 + norm * (1.0 - sigma)))
        out_ref[col] = grad
        state[0] = state[0] + jnp.sum(grad, axis=0)
        state[1] = state[1] + jnp.sum(grad * hat, axis=0)

    for a, b in pieces(cols, 8):
        convolve(low_ref, pair_ref, True, rows, a, b, take)
        mover.put(out_ref.at[a:b], grad_far.at[a:b])
    plain, cross = state
    half = images // 2
    pay_ref[0:half] = pack_pair(group_total(plain * gain), group_total(cross * gain))
    rest = [jnp.sum(v, axis=0, keepdims=True) for v in (cross, plain)]
    short = pay_ref.shape[0] - half - 2
    pay_ref[half:] = jnp.concatenate(rest + [jnp.zeros((short, chans), F32)], axis=0)


CODE = 32768.0


def exponents(values):
    most = jnp.clip(jnp.max(jnp.abs(values), axis=0, keepdims=True), 1e-30, 1e30)
    return jnp.ceil(jnp.log2(most) + 2e-3)


def two_to(powers):
    powers = powers.astype(jnp.int32)
    first = powers >> 1
    made = None
    for part in (first, powers - first):
        shifted = part + 64
        for bit in range(7):
            factor = jnp.where((shifted >> bit) & 1 == 1, 2.0 ** (1 << bit), 1.0)
            if bit == 0:
                piece = factor * 2.0**-64
            else:
                piece = piece * factor
        made = piece if made is None else made * piece
    return made


def pack_terms(
    keep_one_ref, came_one_ref, keep_two_ref, came_two_ref, out_far, token_ref,
    one_ref, two_ref, extra_ref, rest_ref, out_ref, mover, extras_one, extras_two,
):
    chips, rows, chans = out_ref.shape
    taps = 9 * (chans // 2)
    share = -(-taps // chips)
    more = -(-(extras_one + extras_two) // chips)
    extra_ref[...] = jnp.zeros(extra_ref.shape, F32)
    one_ref[...] = keep_one_ref[...] + came_one_ref[...]
    two_ref[...] = keep_two_ref[...] + came_two_ref[...]
    extra_ref[0:extras_two] = two_ref[taps : taps + extras_two]
    extra_ref[extras_two : extras_two + extras_one] = one_ref[taps : taps + extras_one]
    token_ref[...] = extra_ref[0:8]
    powers = []
    for ref, count in ((one_ref, taps), (two_ref, taps), (extra_ref, extra_ref.shape[0])):
        values = ref[0:count]
        power = exponents(values)
        powers.append(power)
        scaled = values * (two_to(-power) * CODE)
        code = jnp.round(scaled)
        ref[0:count] = code
        if ref is extra_ref:
            rest_ref[...] = jnp.round((scaled - code) * CODE)
    short = rows - 2 * share - 2 * more - 3
    pad = [jnp.zeros((short, chans), F32)] if short else []
    for chip in range(chips):
        a, b = chip * share, min((chip + 1) * share, taps)
        mine = []
        for ref in (one_ref, two_ref):
            if a < b:
                mine.append(ref[a:b])
            if max(b - a, 0) < share:
                mine.append(jnp.zeros((share - max(b - a, 0), chans), F32))
        for ref in (extra_ref, rest_ref):
            mine.append(ref[chip * more : (chip + 1) * more])
        whole = jnp.concatenate(mine + powers + pad, axis=0)
        out_ref[chip] = whole.astype(jnp.int32).astype(jnp.int16)
    mover.put(out_ref, out_far)


def unpack_terms(gathered_ref, share, more):
    chips, rows, chans = gathered_ref.shape
    row = lax.broadcasted_iota(jnp.int32, (rows, chans), 0)
    base = 2 * share + 2 * more
    total = jnp.zeros((rows, chans), F32)
    blocks = [gathered_ref[chip].astype(jnp.int32).astype(F32) for chip in range(chips)]
    every = two_to(jnp.concatenate([block[base : base + 3] for block in blocks], axis=0)) * (1.0 / CODE)
    for chip, block in enumerate(blocks):
        scales = every[3 * chip : 3 * chip + 3]
        scale = jnp.where(row < share, scales[0:1], jnp.where(row < 2 * share, scales[1:2], scales[2:3]))
        scale = jnp.where(row < 2 * share + more, scale, scale * (1.0 / CODE))
        total = total + block * scale
    extra = total[2 * share : 2 * share + more] + total[2 * share + more : base]
    return total[0 : 2 * share], extra


def two_terms(values):
    high = values.astype(BF16).astype(F32)
    return [high, values - high]


def add_terms(gathered_ref, pay_ref, came_ref, out_far, out_ref, mover, more, whole):
    chips, rows, chans = gathered_ref.shape
    shares, extra = unpack_terms(gathered_ref, -(-9 * (chans // 2) // chips), more)
    every = [shares] + two_terms(extra) + two_terms(pay_ref[0:whole] + came_ref[0:whole])
    short = out_ref.shape[1] - sum(v.shape[0] for v in every)
    if short:
        every.append(jnp.zeros((short, chans), F32))
    out_ref[...] = jnp.broadcast_to(jnp.concatenate(every, axis=0).astype(BF16)[None], out_ref.shape)
    mover.put(out_ref, out_far)


def sums_of(own_ref, at, whole):
    total = own_ref[0].astype(F32)
    for chip in range(1, own_ref.shape[0]):
        total = total + own_ref[chip].astype(F32)
    return total[at : at + whole] + total[at + whole : at + 2 * whole]


def three_terms(values):
    high = values.astype(BF16)
    rest = values - high.astype(F32)
    mid = rest.astype(BF16)
    low = (rest - mid.astype(F32)).astype(BF16)
    return jnp.concatenate([high, mid, low], axis=0)


def spread_out(own_ref, other_ref, one_far, two_far, one_ref, two_ref, half_ref, mover):
    chips, rows, chans = own_ref.shape
    half = chans // 2
    taps = 9 * half
    share = -(-taps // chips)
    core = lax.axis_index("ha") % 2
    for at, (out_ref, far) in enumerate(((one_ref, one_far), (two_ref, two_far))):
        for source, place in ((own_ref, core), (other_ref, 1 - core)):
            for chip in range(chips):
                piece = source[chip].astype(F32)[at * share : (at + 1) * share]
                half_ref[chip * share : (chip + 1) * share] = piece
            for tap in range(9):
                rows_at = pl.ds(pl.multiple_of(place * half, half), half)
                out_ref[tap, rows_at] = half_ref[tap * half : (tap + 1) * half]
        mover.put(out_ref, far)


def last_grads(
    weight_far, grad_ref, xt_ref, c_ref, own_ref, stat_ref, gain_one_ref, gain_two_ref, bias_two_ref, film_ref, ints_ref, text_ref,
    out_far, weight_grad_far, text_grad_far, bias_ref, *refs, more, whole,
):
    *vec_refs, weight_ref, out_ref, weight_grad_ref, text_grad_ref, extra_ref, mover = refs
    images, rows, cols, chans = out_ref.shape
    chips = own_ref.shape[0]
    load = mover.start(weight_far, weight_ref)
    share = -(-9 * (chans // 2) // chips)
    start = 2 * share
    for chip in range(chips):
        piece = own_ref[chip].astype(F32)
        extra_ref[chip * more : (chip + 1) * more] = piece[start : start + more] + piece[start + more : start + 2 * more]
    plain = extra_ref[0:images]
    cross = extra_ref[images : 2 * images]
    mover.ready()
    scale = 1.0 + film_ref[:, 0:chans]
    scale_grad = gain_two_ref[...].astype(F32) * cross + bias_two_ref[...].astype(F32) * plain
    film_grad = jnp.concatenate([scale_grad, plain], axis=1)
    bias_ref[...] = jnp.sum(film_grad, axis=0, keepdims=True)
    sums = sums_of(own_ref, start + 2 * more, whole)
    vec_refs[0][...] = jnp.sum(scale * cross, axis=0, keepdims=True)
    vec_refs[1][...] = jnp.sum(scale * plain, axis=0, keepdims=True)
    for at, row in enumerate((extra_ref[2 * images : 2 * images + 1], extra_ref[2 * images + 1 : 2 * images + 2])):
        vec_refs[2 + at][...] = row
    vec_refs[4][...] = sums[whole - 2 : whole - 1]
    vec_refs[5][...] = sums[whole - 1 : whole]
    terms = three_terms(film_grad)
    ints = ints_ref.shape[1]

    depth = weight_grad_ref.shape[0]
    for at in range(0, depth, 512):
        if at < ints:
            act = ints_ref[:, at : at + 512]
        else:
            embed = text_ref[:, at - ints : at - ints + 512].astype(F32)
            act = (embed * sigmoid(embed)).astype(BF16)
        weight_grad_ref[at : at + 512] = lax.dot_general(
            jnp.concatenate([act, act, act], axis=0), terms, (((0,), (0,)), ((), ())), preferred_element_type=F32
        )
        mover.put(weight_grad_ref.at[at : at + 512], weight_grad_far.at[at : at + 512])

    count = lax.axis_size("ha") * lax.axis_size("wa") * rows * cols * (chans // GROUPS)
    packed = sums[0 : images // 2] * (1.0 / count)
    plain = unpack_at(packed, 0)
    cross = unpack_at(packed, 1)
    mean = stat_ref[0]
    inv = stat_ref[1]
    gain = gain_one_ref[...].astype(F32)
    for a, b in pieces(rows, 2):
        for row in range(a, b):
            hat = (xt_ref[:, row].astype(F32) - mean) * inv
            path = jnp.swapaxes(inv * (grad_ref[:, row] * gain - plain - hat * cross), 0, 1)
            out_ref[:, row] = (c_ref[:, row].astype(F32) * INV_ROOT + path).astype(BF16)
        mover.put(out_ref.at[:, a:b], out_far.at[:, a:b])

    load.wait()
    for at in range(ints, depth, 512):
        embed = text_ref[:, at - ints : at - ints + 512].astype(F32)
        sigma = sigmoid(embed)
        made = lax.dot_general(
            terms, weight_ref[at : at + 512], (((1,), (1,)), ((), ())), preferred_element_type=F32
        )
        cond_grad = made[0:images] + made[images : 2 * images] + made[2 * images :]
        text_grad_ref[:, at - ints : at - ints + 512] = cond_grad * (sigma * (1.0 + embed * (1.0 - sigma)))
    mover.put(text_grad_ref, text_grad_far)


def to_all(payload):
    return lax.all_to_all(payload, AXES, 0, 0)


def to_chips(payload):
    tall, wide = lax.axis_size("ha"), lax.axis_size("wa")
    groups = [[h * wide + w for h in range(core, tall, 2) for w in range(wide)] for core in range(2)]
    return lax.all_to_all(payload, AXES, 0, 0, axis_index_groups=groups)


def to_sibling(payload):
    return lax.ppermute(payload, "ha", [(i, i ^ 1) for i in range(lax.axis_size("ha"))])


def pair_exchange(one, other, axis):
    count = lax.axis_size(axis)
    pairs = [(i, (i + 1 if i % 2 else i - 1) % count) for i in range(count)]
    if axis == "wa":
        pairs = [(i, min(max(j, 0), count - 1) if abs(i - j) == 1 else i) for i, j in pairs]
    one = lax.ppermute(one, axis, [(i, i ^ 1) for i in range(count)])
    return one, lax.ppermute(other, axis, pairs)


def side_halo(sides, near, following, after=()):
    four, rows, images, chans = sides.shape
    edge = shaped((2, rows + 4, images, chans), sides.dtype)
    one, other = kernel_call(
        edge_columns, near=(sides, near, following), near_out=(edge, edge), cost=0.4, after=after, limit=16
    )
    return pair_exchange(one, other, "wa"), one


def local(
    block_input,
    timesteps,
    aug_levels,
    text_pooled,
    gain_one,
    bias_one,
    conv_one,
    conv_one_bias,
    gain_two,
    bias_two,
    film_weight,
    film_bias,
    conv_two,
    conv_two_bias,
    cotangent,
):
    images, rows, cols, chans = block_input.shape
    parts = lax.axis_size("ha") * lax.axis_size("wa")
    chips = parts // 2
    half = images // 2
    gain_one, bias_one, conv_one_bias, gain_two, bias_two, conv_two_bias = (
        v.reshape(1, chans) for v in (gain_one, bias_one, conv_one_bias, gain_two, bias_two, conv_two_bias)
    )
    freqs = np.exp(-math.log(10000.0) * np.arange(TEMB // 2) / (TEMB // 2)).astype(np.float32)[None]
    payload = shaped((parts, half, chans), F32)
    per_image = shaped((images, chans), F32)
    two_images = shaped((2, images, chans), F32)
    block = shaped((cols, rows, images, chans), BF16)
    block_wide = shaped((cols, rows, images, chans), F32)
    rim = shaped((cols + 2, rows + 2, images, chans), BF16)
    rim_wide = shaped((cols + 2, rows + 2, images, chans), F32)
    far_rim = shaped((cols + 4, rows + 4, images, chans), BF16)
    given = shaped((images, rows, cols, chans), BF16)
    pair = pltpu.VMEM((12 * chans, 2 * chans), BF16)
    pair_back = pltpu.VMEM((2 * chans, 12 * chans), BF16)

    sides = shaped((4, rows, images, chans), BF16)
    row_halo = shaped((cols, 2, images, chans), BF16)
    xt, x_near, x_next, x_sides, moments = kernel_call(
        prepare_x, far=(block_input,), far_out=(block,),
        near_out=(row_halo, row_halo, sides, shaped((half, chans), F32)),
        scratch=buffers(given, block), sems=16, cost=2.3,
    )
    x_near, x_next = pair_exchange(x_near, x_next, "ha")
    gt, pay_one, g_near, g_next, g_sides, kbias_two_local = kernel_call(
        prepare_g, far=(cotangent,), near=(moments,), far_out=(block, payload),
        near_out=(row_halo, row_halo, sides), tiny_out=(per_image,),
        scratch=buffers(given, block, payload), sems=16, cost=2.0,
    )
    moments_one = to_all(pay_one)
    x_cols, x_edge = side_halo(x_sides, x_near, x_next)
    g_near, g_next = pair_exchange(g_near, g_next, "ha")

    film_bias = film_bias.reshape(1, 2 * chans)
    act_one, mid, pay_two, stat_one = kernel_call(
        first_half, far=(xt, conv_one), near=(x_near, x_next, *x_cols, moments_one),
        tiny=(gain_one, bias_one, conv_one_bias),
        far_out=(far_rim, rim_wide, payload), tiny_out=(two_images,),
        scratch=buffers(xt, conv_one, far_rim, rim_wide, payload) + (pair,), sems=16, cost=5.5,
        after=(film_bias,),
    )
    moments_two = to_all(pay_two)
    g_cols, _ = side_halo(g_sides, g_near, g_next, after=(stat_one,))
    act_two_grad, film, act_ints = kernel_call(
        back_two, far=(gt, conv_two, film_weight), near=(g_near, g_next, *g_cols),
        tiny=(text_pooled, film_bias, freqs), scalars=(timesteps, aug_levels),
        far_out=(rim_wide,), tiny_out=(shaped((images, 2 * chans), F32), shaped((images, 2 * TEMB), BF16)),
        scratch=buffers(gt, conv_two, film_weight, far_rim, rim_wide) + (pair_back,), sems=16, cost=5.0,
    )
    act_two, pre_two_grad, pay_three, sums_two, stat_two = kernel_call(
        second_norm, far=(mid, act_two_grad), near=(moments_two,), tiny=(gain_two, bias_two, film),
        far_out=(rim, rim, payload), tiny_out=(two_images, two_images),
        scratch=buffers(rim_wide, rim_wide, rim, rim, payload), sems=24, cost=3.2,
    )
    moments_three = to_all(pay_three)

    taps = 9 * (chans // 2)
    share = -(-taps // chips)
    extras_two = 2 * images + 1
    extras_one = 1
    halves_two = shaped((taps + 2 * images + 8, chans), F32)
    halves_one = shaped((taps + 8, chans), F32)
    keep_two, send_two = kernel_call(
        kernel_two, far=(act_two, gt), tiny=(sums_two, kbias_two_local), far_out=(halves_two, halves_two),
        scratch=buffers(act_two, gt, halves_two, halves_two), sems=4, cost=3.0,
    )
    came_two = to_sibling(send_two)
    low, keep_one, send_one, keep_two = kernel_call(
        middle_grad, far=(mid, pre_two_grad, act_one, keep_two), near=(moments_three,), tiny=(stat_two, gain_two, film),
        far_out=(rim,), near_out=(halves_one, halves_one, halves_two),
        scratch=buffers(mid, pre_two_grad, act_one, rim), sems=24, cost=6.0,
    )
    came_one = to_sibling(send_one)
    more = -(-(extras_one + extras_two) // chips)
    terms_shape = shaped((chips, -(-(2 * share + 2 * more + 3) // 8) * 8, chans), jnp.int16)
    extra_shape = shaped((-(-chips * more // 8) * 8, chans), F32)
    terms, token = kernel_call(
        functools.partial(pack_terms, extras_one=extras_one, extras_two=extras_two),
        near=(keep_one, came_one, keep_two, came_two), far_out=(terms_shape,), near_out=(shaped((8, chans), F32),),
        scratch=buffers(halves_one, halves_two, extra_shape, extra_shape, terms_shape),
        sems=3, cost=1.0,
    )
    gathered = to_chips(terms)
    whole = half + 2
    norm_one_grad, pay_four = kernel_call(
        back_one, far=(low, xt, conv_one), tiny=(stat_one, gain_one, bias_one), far_out=(block_wide,),
        near_out=(shaped((2 * half, chans), F32),),
        scratch=buffers(rim, block, conv_one, block_wide) + (pair_back,), sems=16, cost=5.0,
        after_near=(to_sibling(token),),
    )
    came_four = to_sibling(pay_four)
    (mixed,) = kernel_call(
        mix, far=(act_two, conv_two, xt), tiny=(conv_two_bias,), far_out=(given,),
        scratch=buffers(act_two, conv_two, xt, block_wide, given) + (pair,), sems=8, cost=3.6, after_near=(pay_four,),
    )
    shares_shape = shaped((chips, -(-(2 * share + 2 * more + 2 * whole) // 8) * 8, chans), BF16)
    (shares,) = kernel_call(
        functools.partial(add_terms, more=more, whole=whole),
        near=(gathered, pay_four, came_four), far_out=(shares_shape,),
        scratch=buffers(shares_shape), sems=1, cost=1.0, after=(mixed,),
    )
    own_half = to_chips(shares)
    other_half = to_sibling(own_half)
    weight_grad = shaped(film_weight.shape, F32)
    text_shape = shaped(text_pooled.shape, F32)
    row = shaped((1, chans), F32)
    input_grad, film_weight_grad, text_grad, film_bias_grad, *vec_grads = kernel_call(
        functools.partial(last_grads, more=more, whole=whole),
        far=(film_weight,),
        near=(norm_one_grad, xt, cotangent, own_half, stat_one, gain_one, gain_two, bias_two, film, act_ints, text_pooled),
        far_out=(given, weight_grad, text_shape), tiny_out=(shaped((1, 2 * chans), F32),) + (row,) * 6,
        scratch=buffers(film_weight, given, weight_grad, text_shape)
        + (pltpu.VMEM((-(-chips * more // 8) * 8, chans), F32),),
        sems=32, cost=6.0, limit=24,
    )
    full = shaped((9, chans, chans), F32)
    kernel_one_grad, kernel_two_grad = kernel_call(
        spread_out, near=(own_half, other_half), far_out=(full, full),
        scratch=buffers(full, full, shaped((chips * share, chans), F32)), sems=2, cost=2.0, after=(input_grad,), limit=24,
    )
    return (
        mixed,
        input_grad,
        text_grad,
        vec_grads[4].reshape(chans),
        vec_grads[5].reshape(chans),
        kernel_one_grad.reshape(3, 3, chans, chans),
        vec_grads[3].reshape(chans),
        vec_grads[0].reshape(chans),
        vec_grads[1].reshape(chans),
        film_weight_grad,
        film_bias_grad.reshape(2 * chans),
        kernel_two_grad.reshape(3, 3, chans, chans),
        vec_grads[2].reshape(chans),
    )


def solution(mesh):
    split = P(None, "ha", "wa", None)
    return jax.shard_map(
        local,
        mesh=mesh,
        in_specs=(split,) + (P(),) * 13 + (split,),
        out_specs=(split, split) + (P(),) * 11,
        check_vma=False,
    )
```

profile of v0, /device:TPU:1, one launch (start us, length us, event | category | flops | bytes accessed | tf_op | source)
XLA Modules:
  0.0 110.7 jit_solution(13604543655856642868)
XLA Ops:
  0.6 2.7 %prepare_x.1 = (bf16[32,8,16,128]{3,2,1,0:T(8,128)(2,1)}, bf16[32,2,16,128]{3,2,1,0:T(8,128)(2,1)S(1)}, bf16[32,2,16,128]{3,2,1,0:T(8,128)(2,1)S(1)}, bf16[4,8,16,128]{3,2,1,0:T(8,128)(2,1)S(1)}, f32[8,128]{1,0:T(8,128)S(1)}) custom-call(bf16[16,8,32,128]{3,2,1,0:T(8,128)(2,1)} %refs_0_.3), custom_call_target="tpu_custom_call" | custom-call | flops 2529999872 | tf_op jit(solution)/shard_map/prepare_x/pallas_call | solution.py:57
  3.5 2.6 %collective-permute-start.1 = (bf16[32,2,16,128]{3,2,1,0:T(8,128)(2,1)S(1)}, bf16[32,2,16,128]{3,2,1,0:T(8,128)(2,1)S(1)}, u32[]{:S(2)}, u32[]{:S(2)}) collective-permute-start(bf16[32,2,16,128]{3,2,1,0:T(8,128)(2,1)S(1)} %get-tuple-element.64), channel_id=1, source_target_pairs={{0,28},{4,8},{8,4},{12,16},{16,12},{20,24},{24,20},{28,0},{1,29},{... | collective-permute-start | bytes 786440 | tf_op jit(solution)/shard_map/ppermute | solution.py:859
  6.1 2.6 %prepare_g.1 = (bf16[32,8,16,128]{3,2,1,0:T(8,128)(2,1)}, f32[32,8,128]{2,1,0:T(8,128)}, bf16[32,2,16,128]{3,2,1,0:T(8,128)(2,1)S(1)}, bf16[32,2,16,128]{3,2,1,0...) custom-call(bf16[16,8,32,128]{3,2,1,0:T(8,128)(2,1)} %refs_3_.1, ...), custom_call_target="tpu_custom_call" | custom-call | flops 2200000000 | tf_op jit(solution)/shard_map/prepare_g/pallas_call | solution.py:57
  8.7 5.1 %all-to-all-start = ((f32[32,8,128]{2,1,0:T(8,128)}), f32[32,8,128]{2,1,0:T(8,128)S(1)}, u32[]{:S(2)}, u32[]{:S(2)}) async-start(f32[32,8,128]{2,1,0:T(8,128)} %get-tuple-element.69), calls=%async_computation | async-start | bytes 262144 | tf_op jit(solution)/shard_map/all_to_all | solution.py:840
  13.9 1.5 %collective-permute-start.2 = (bf16[2,12,16,128]{3,2,1,0:T(8,128)(2,1)S(1)}, bf16[2,12,16,128]{3,2,1,0:T(8,128)(2,1)S(1)}, u32[]{:S(2)}, u32[]{:S(2)}) collective-permute-start(bf16[2,12,16,128]{3,2,1,0:T(8,128)(2,1)S(1)} %get-tuple-element.66), channel_id=1, source_target_pairs={{0,1},{1,0},{2,3},{3,2},{4,5},{5,4},{6,7},{7,6},{8,9},{9,8},{10,11... | collective-permute-start | bytes 294920 | tf_op jit(solution)/shard_map/ppermute | solution.py:858
  15.3 0.7 collective-permute-start.3
  16.0 0.7 collective-permute-start.4
  16.7 1.1 %collective-permute-start.5 = (bf16[32,2,16,128]{3,2,1,0:T(8,128)(2,1)S(1)}, bf16[32,2,16,128]{3,2,1,0:T(8,128)(2,1)S(1)}, u32[]{:S(2)}, u32[]{:S(2)}) collective-permute-start(bf16[32,2,16,128]{3,2,1,0:T(8,128)(2,1)S(1)} %get-tuple-element.73), channel_id=1, source_target_pairs={{0,28},{4,8},{8,4},{12,16},{16,12},{20,24},{24,20},{28,0},{1,29},{... | collective-permute-start | bytes 786440 | tf_op jit(solution)/shard_map/ppermute | solution.py:859
  18.4 2.7 %all-to-all-done.refs_6_ = f32[32,8,128]{2,1,0:T(8,128)S(1)} async-done(((f32[32,8,128]{2,1,0:T(8,128)}), f32[32,8,128]{2,1,0:T(8,128)S(1)}, u32[]{:S(2)}, u32[]{:S(2)}) %all-to-all-start) | async-done | bytes 131104 | tf_op jit(solution)/shard_map/all_to_all | solution.py:840
  21.1 5.6 %first_half.1 = (bf16[36,12,16,128]{3,2,1,0:T(8,128)(2,1)}, f32[34,10,16,128]{3,2,1,0:T(8,128)}, f32[32,8,128]{2,1,0:T(8,128)}, f32[2,16,128]{2,1,0:T(8,128)}) custom-call(bf16[32,8,16,128]{3,2,1,0:T(8,128)(2,1)} %get-tuple-element.62.refs_0_.refs_1_.refs_2_, bf16[3,3,128,128]{3,2,1,0:T(8,128)(2,1)} %refs_2_.3, ...), custom_call_target="tpu_custom_call" | custom-call | flops 6049999872 | tf_op jit(solution)/shard_map/first_half/pallas_call | solution.py:57
  26.8 2.5 %collective-permute-start.6 = (bf16[2,12,16,128]{3,2,1,0:T(8,128)(2,1)S(1)}, bf16[2,12,16,128]{3,2,1,0:T(8,128)(2,1)S(1)}, u32[]{:S(2)}, u32[]{:S(2)}) collective-permute-start(bf16[2,12,16,128]{3,2,1,0:T(8,128)(2,1)S(1)} %get-tuple-element.76), channel_id=1, source_target_pairs={{0,1},{1,0},{2,3},{3,2},{4,5},{5,4},{6,7},{7,6},{8,9},{9,8},{10,11... | collective-permute-start | bytes 294920 | tf_op jit(solution)/shard_map/ppermute | solution.py:858
  29.2 0.7 collective-permute-start.7
  29.9 5.2 %all-to-all-start.1 = ((f32[32,8,128]{2,1,0:T(8,128)}), f32[32,8,128]{2,1,0:T(8,128)S(1)}, u32[]{:S(2)}, u32[]{:S(2)}) async-start(f32[32,8,128]{2,1,0:T(8,128)} %get-tuple-element.79), calls=%async_computation.1 | async-start | bytes 262144 | tf_op jit(solution)/shard_map/all_to_all | solution.py:840
  35.1 6.1 %back_two.1 = (f32[34,10,16,128]{3,2,1,0:T(8,128)}, f32[16,256]{1,0:T(8,128)}, bf16[16,512]{1,0:T(8,128)(2,1)}) custom-call(bf16[32,8,16,128]{3,2,1,0:T(8,128)(2,1)} %get-tuple-element.71.refs_0_.refs_1_, bf16[3,3,128,128]{3,2,1,0:T(8,128)(2,1)} %refs_1_.5, bf16[4608,256]{1,0:T(8,128)(2,1)} %refs_0_.5, ...), custom_call_target="tpu_custom_call" | custom-call | flops 5500000256 | tf_op jit(solution)/shard_map/back_two/pallas_call | solution.py:57
  41.3 1.1 %all-to-all-done.1.refs_2_ = f32[32,8,128]{2,1,0:T(8,128)S(1)} async-done(((f32[32,8,128]{2,1,0:T(8,128)}), f32[32,8,128]{2,1,0:T(8,128)S(1)}, u32[]{:S(2)}, u32[]{:S(2)}) %all-to-all-start.1) | async-done | bytes 131104 | tf_op jit(solution)/shard_map/all_to_all | solution.py:840
  42.4 4.4 %second_norm.1 = (bf16[34,10,16,128]{3,2,1,0:T(8,128)(2,1)}, bf16[34,10,16,128]{3,2,1,0:T(8,128)(2,1)}, f32[32,8,128]{2,1,0:T(8,128)}, f32[2,16,128]{2,1,0:T(8,128)}, f32[2,16,128]{2,1,0:T(8,128)}) custom-call(f32[34,10,16,128]{3,2,1,0:T(8,128)} %get-tuple-element.70.refs_0_, f32[34,10,16,128]{3,2,1,0:T(8,128)} %get-tuple-element.78.refs_1_, ...), custom_call_target="tpu_custom_call" | custom-call | flops 3520000000 | tf_op jit(solution)/shard_map/second_norm/pallas_call | solution.py:57
  46.8 4.7 %all-to-all-start.2 = ((f32[32,8,128]{2,1,0:T(8,128)}), f32[32,8,128]{2,1,0:T(8,128)S(1)}, u32[]{:S(2)}, u32[]{:S(2)}) async-start(f32[32,8,128]{2,1,0:T(8,128)} %get-tuple-element.87), calls=%async_computation.2 | async-start | bytes 262144 | tf_op jit(solution)/shard_map/all_to_all | solution.py:840
  51.5 4.2 %kernel_two.1 = (f32[616,128]{1,0:T(8,128)}, f32[616,128]{1,0:T(8,128)}) custom-call(bf16[34,10,16,128]{3,2,1,0:T(8,128)(2,1)} %get-tuple-element.81.refs_0_, bf16[32,8,16,128]{3,2,1,0:T(8,128)(2,1)} %get-tuple-element.71.refs_0_.refs_1_, f32[2,16,128]{2,1,0:T(8,128)} %get-tuple-element.84.refs_2_, f32[16,128]{1,0:T(8,128)} %get-tuple-element.85.refs_3_), custom_call_target="tpu_custom_call" | custom-call | flops 3300000000 | tf_op jit(solution)/shard_map/kernel_two/pallas_call | solution.py:57
  56.1 2.8 %all-to-all-done.2.refs_4_ = f32[32,8,128]{2,1,0:T(8,128)S(1)} async-done(((f32[32,8,128]{2,1,0:T(8,128)}), f32[32,8,128]{2,1,0:T(8,128)S(1)}, u32[]{:S(2)}, u32[]{:S(2)}) %all-to-all-start.2) | async-done | bytes 131104 | tf_op jit(solution)/shard_map/all_to_all | solution.py:840
  58.8 4.9 %middle_grad.1 = (bf16[34,10,16,128]{3,2,1,0:T(8,128)(2,1)}, f32[584,128]{1,0:T(8,128)S(1)}, f32[584,128]{1,0:T(8,128)S(1)}, f32[616,128]{1,0:T(8,128)S(1)}) custom-call(f32[34,10,16,128]{3,2,1,0:T(8,128)} %get-tuple-element.70.refs_0_, bf16[34,10,16,128]{3,2,1,0:T(8,128)(2,1)} %get-tuple-element.82.refs_1_, ...), custom_call_target="tpu_custom_call" | custom-call | flops 6600000000 | tf_op jit(solution)/shard_map/middle_grad/pallas_call | solution.py:57
  63.8 1.4 %collective-permute-start.8 = (f32[584,128]{1,0:T(8,128)S(1)}, f32[584,128]{1,0:T(8,128)S(1)}, u32[]{:S(2)}, u32[]{:S(2)}) collective-permute-start(f32[584,128]{1,0:T(8,128)S(1)} %get-tuple-element.91), channel_id=1, source_target_pairs={{0,4},{4,0},{8,12},{12,8},{16,20},{20,16},{24,28},{28,24},{1,5},{5... | collective-permute-start | bytes 897032 | tf_op jit(solution)/shard_map/ppermute | solution.py:850
  65.2 1.2 %collective-permute-done.8.refs_1_ = f32[584,128]{1,0:T(8,128)S(1)} collective-permute-done((f32[584,128]{1,0:T(8,128)S(1)}, f32[584,128]{1,0:T(8,128)S(1)}, u32[]{:S(2)}, u32[]{:S(2)}) %collective-permute-start.8) | collective-permute-done | bytes 299040 | tf_op jit(solution)/shard_map/ppermute | solution.py:850
  66.4 1.1 pack_terms.1
  67.9 3.5 %all-to-all-start.3 = ((s16[16,88,128]{2,1,0:T(8,128)(2,1)}), s16[16,88,128]{2,1,0:T(8,128)(2,1)S(1)}, u32[]{:S(2)}, u32[]{:S(2)}) async-start(s16[16,88,128]{2,1,0:T(8,128)(2,1)} %get-tuple-element.97), calls=%async_computation.3 | async-start | bytes 720896 | tf_op jit(solution)/shard_map/all_to_all | solution.py:846
  71.5 5.5 %back_one.1 = (f32[32,8,16,128]{3,2,1,0:T(8,128)}, f32[16,128]{1,0:T(8,128)S(1)}) custom-call(bf16[34,10,16,128]{3,2,1,0:T(8,128)(2,1)} %get-tuple-element.89.refs_0_, bf16[32,8,16,128]{3,2,1,0:T(8,128)(2,1)} %get-tuple-element.62.refs_0_.refs_1_.refs_2_, bf16[3,3,128,128]{3,2,1,0:T(8,128)(2,1)} %refs_2_.3, f32[2,16,128]{2,1,0:T(8,128)} %get-tuple-element.75.refs_3_.refs_5_, ...), custom_call_target="tpu_custom_call" | custom-call | flops 5500000256 | tf_op jit(solution)/shard_map/back_one/pallas_call | solution.py:57
  77.3 4.7 %mix.1.refs_3_ = bf16[16,8,32,128]{3,2,1,0:T(8,128)(2,1)} custom-call(bf16[34,10,16,128]{3,2,1,0:T(8,128)(2,1)} %get-tuple-element.81.refs_0_, bf16[3,3,128,128]{3,2,1,0:T(8,128)(2,1)} %refs_1_.5, bf16[32,8,16,128]{3,2,1,0:T(8,128)(2,1)} %get-tuple-element.62.refs_0_.refs_1_.refs_2_, bf16[1,128]{1,0:T(2,128)(2,1)} %bitcast.26, ...), custom_call_target="tpu_custom_call" | custom-call | flops 3960000000 | tf_op jit(solution)/shard_map/mix/pallas_call | solution.py:57
  82.1 1.8 %all-to-all-done.3.refs_0_ = s16[16,88,128]{2,1,0:T(8,128)(2,1)S(1)} async-done(((s16[16,88,128]{2,1,0:T(8,128)(2,1)}), s16[16,88,128]{2,1,0:T(8,128)(2,1)S(1)}, u32[]{:S(2)}, u32[]{:S(2)}) %all-to-all-start.3) | async-done | bytes 360480 | tf_op jit(solution)/shard_map/all_to_all | solution.py:846
  83.8 1.0 add_terms.1
  84.8 18.6 %all_to_all.25.refs_4_.refs_0_ = bf16[16,104,128]{2,1,0:T(8,128)(2,1)S(1)} all-to-all(bf16[16,104,128]{2,1,0:T(8,128)(2,1)} %add_terms.1), channel_id=1, replica_groups={{0,1,2,3,8,9,10,11,16,17,18,19,24,25,26,27},{4,5,6,7,12,13,14,15,20,21,..., dimensions={0} | all-to-all | bytes 851968 | tf_op jit(solution)/shard_map/all_to_all | solution.py:846
  103.4 1.5 %collective-permute-start.12 = (bf16[16,104,128]{2,1,0:T(8,128)(2,1)S(1)}, bf16[16,104,128]{2,1,0:T(8,128)(2,1)S(1)}, u32[]{:S(2)}, u32[]{:S(2)}) collective-permute-start(bf16[16,104,128]{2,1,0:T(8,128)(2,1)S(1)} %all_to_all.25.refs_4_.refs_0_), channel_id=1, source_target_pairs={{0,4},{4,0},{8,12},{12,8},{16,20},{20,16},{24,28},{28,24},{1,5},{5... | collective-permute-start | bytes 1277960 | tf_op jit(solution)/shard_map/ppermute | solution.py:850
  104.9 4.4 %last_grads.1 = (bf16[16,8,32,128]{3,2,1,0:T(8,128)(2,1)}, f32[4608,256]{1,0:T(8,128)}, f32[16,4096]{1,0:T(8,128)}, f32[1,256]{1,0:T(1,128)}, f32[1,128]{1,0:T(1...) custom-call(bf16[4608,256]{1,0:T(8,128)(2,1)} %refs_0_.5, ...), custom_call_target="tpu_custom_call" | custom-call | flops 6600000000 | tf_op jit(solution)/shard_map/last_grads/pallas_call | solution.py:57
  109.4 1.1 %spread_out.1 = (f32[9,128,128]{2,1,0:T(8,128)}, f32[9,128,128]{2,1,0:T(8,128)}) custom-call(bf16[16,104,128]{2,1,0:T(8,128)(2,1)S(1)} %all_to_all.25.refs_4_.refs_0_, bf16[16,104,128]{2,1,0:T(8,128)(2,1)S(1)} %collective-permute-done.12.refs_1_, bf16[16,8,32,128]{3,2,1,0:T(8,128)(2,1)} %get-tuple-element.50.refs_2_), custom_call_target="tpu_custom_call" | custom-call | flops 2200000000 | tf_op jit(solution)/shard_map/spread_out/pallas_call | solution.py:57
  (45 shorter events, 1.9 us)
Async XLA Ops:
  3.4 10.4 %collective-permute-start = (bf16[32,2,16,128]{3,2,1,0:T(8,128)(2,1)S(1)}, bf16[32,2,16,128]{3,2,1,0:T(8,128)(2,1)S(1)}, u32[]{:S(2)}, u32[]{:S(2)}) collective-permute-start(bf16[32,2,16,128]{3,2,1,0:T(8,128)(2,1)S(1)} %get-tuple-element.63), channel_id=1, source_target_pairs={{0,4},{4,0},{8,12},{12,8},{16,20},{20,16},{24,28},{28,24},{1,5},{5... | collective-permute-start | bytes 786440 | tf_op jit(solution)/shard_map/ppermute | solution.py:858
  3.5 10.3 %collective-permute-start.1 = (bf16[32,2,16,128]{3,2,1,0:T(8,128)(2,1)S(1)}, bf16[32,2,16,128]{3,2,1,0:T(8,128)(2,1)S(1)}, u32[]{:S(2)}, u32[]{:S(2)}) collective-permute-start(bf16[32,2,16,128]{3,2,1,0:T(8,128)(2,1)S(1)} %get-tuple-element.64), channel_id=1, source_target_pairs={{0,28},{4,8},{8,4},{12,16},{16,12},{20,24},{24,20},{28,0},{1,29},{... | collective-permute-start | bytes 786440 | tf_op jit(solution)/shard_map/ppermute | solution.py:859
  6.1 11.7 %copy-start.12 = (bf16[256]{0:T(256)(128)(2,1)S(1)}, bf16[256]{0:T(256)(128)(2,1)}, u32[]{:S(2)}) copy-start(bf16[256]{0:T(256)(128)(2,1)} %param.27) | copy-start | bytes 1540
  8.7 12.4 %all-to-all-start = ((f32[32,8,128]{2,1,0:T(8,128)}), f32[32,8,128]{2,1,0:T(8,128)S(1)}, u32[]{:S(2)}, u32[]{:S(2)}) async-start(f32[32,8,128]{2,1,0:T(8,128)} %get-tuple-element.69), calls=%async_computation | async-start | bytes 262144 | tf_op jit(solution)/shard_map/all_to_all | solution.py:840
  13.9 7.2 %collective-permute-start.2 = (bf16[2,12,16,128]{3,2,1,0:T(8,128)(2,1)S(1)}, bf16[2,12,16,128]{3,2,1,0:T(8,128)(2,1)S(1)}, u32[]{:S(2)}, u32[]{:S(2)}) collective-permute-start(bf16[2,12,16,128]{3,2,1,0:T(8,128)(2,1)S(1)} %get-tuple-element.66), channel_id=1, source_target_pairs={{0,1},{1,0},{2,3},{3,2},{4,5},{5,4},{6,7},{7,6},{8,9},{9,8},{10,11... | collective-permute-start | bytes 294920 | tf_op jit(solution)/shard_map/ppermute | solution.py:858
  15.3 5.8 %collective-permute-start.3 = (bf16[2,12,16,128]{3,2,1,0:T(8,128)(2,1)S(1)}, bf16[2,12,16,128]{3,2,1,0:T(8,128)(2,1)S(1)}, u32[]{:S(2)}, u32[]{:S(2)}) collective-permute-start(bf16[2,12,16,128]{3,2,1,0:T(8,128)(2,1)S(1)} %get-tuple-element.67), channel_id=1, source_target_pairs={{0,0},{1,2},{2,1},{3,3},{4,4},{5,6},{6,5},{7,7},{8,8},{9,10},{10,9... | collective-permute-start | bytes 294920 | tf_op jit(solution)/shard_map/ppermute | solution.py:859
  16.0 10.7 %collective-permute-start.4 = (bf16[32,2,16,128]{3,2,1,0:T(8,128)(2,1)S(1)}, bf16[32,2,16,128]{3,2,1,0:T(8,128)(2,1)S(1)}, u32[]{:S(2)}, u32[]{:S(2)}) collective-permute-start(bf16[32,2,16,128]{3,2,1,0:T(8,128)(2,1)S(1)} %get-tuple-element.72), channel_id=1, source_target_pairs={{0,4},{4,0},{8,12},{12,8},{16,20},{20,16},{24,28},{28,24},{1,5},{5... | collective-permute-start | bytes 786440 | tf_op jit(solution)/shard_map/ppermute | solution.py:858
  16.7 10.0 %collective-permute-start.5 = (bf16[32,2,16,128]{3,2,1,0:T(8,128)(2,1)S(1)}, bf16[32,2,16,128]{3,2,1,0:T(8,128)(2,1)S(1)}, u32[]{:S(2)}, u32[]{:S(2)}) collective-permute-start(bf16[32,2,16,128]{3,2,1,0:T(8,128)(2,1)S(1)} %get-tuple-element.73), channel_id=1, source_target_pairs={{0,28},{4,8},{8,4},{12,16},{16,12},{20,24},{24,20},{28,0},{1,29},{... | collective-permute-start | bytes 786440 | tf_op jit(solution)/shard_map/ppermute | solution.py:859
  21.1 14.0 %copy-start.2 = (s32[16]{0:T(128)S(1)}, s32[16]{0:T(128)}, u32[]{:S(2)}) copy-start(s32[16]{0:T(128)} %refs_10_.1) | copy-start | bytes 196
  21.1 14.0 %copy-start.3 = (s32[16]{0:T(128)S(1)}, s32[16]{0:T(128)}, u32[]{:S(2)}) copy-start(s32[16]{0:T(128)} %refs_11_.2) | copy-start | bytes 196
  26.8 8.3 %collective-permute-start.6 = (bf16[2,12,16,128]{3,2,1,0:T(8,128)(2,1)S(1)}, bf16[2,12,16,128]{3,2,1,0:T(8,128)(2,1)S(1)}, u32[]{:S(2)}, u32[]{:S(2)}) collective-permute-start(bf16[2,12,16,128]{3,2,1,0:T(8,128)(2,1)S(1)} %get-tuple-element.76), channel_id=1, source_target_pairs={{0,1},{1,0},{2,3},{3,2},{4,5},{5,4},{6,7},{7,6},{8,9},{9,8},{10,11... | collective-permute-start | bytes 294920 | tf_op jit(solution)/shard_map/ppermute | solution.py:858
  29.2 5.8 %collective-permute-start.7 = (bf16[2,12,16,128]{3,2,1,0:T(8,128)(2,1)S(1)}, bf16[2,12,16,128]{3,2,1,0:T(8,128)(2,1)S(1)}, u32[]{:S(2)}, u32[]{:S(2)}) collective-permute-start(bf16[2,12,16,128]{3,2,1,0:T(8,128)(2,1)S(1)} %get-tuple-element.77), channel_id=1, source_target_pairs={{0,0},{1,2},{2,1},{3,3},{4,4},{5,6},{6,5},{7,7},{8,8},{9,10},{10,9... | collective-permute-start | bytes 294920 | tf_op jit(solution)/shard_map/ppermute | solution.py:859
  29.9 12.5 %all-to-all-start.1 = ((f32[32,8,128]{2,1,0:T(8,128)}), f32[32,8,128]{2,1,0:T(8,128)S(1)}, u32[]{:S(2)}, u32[]{:S(2)}) async-start(f32[32,8,128]{2,1,0:T(8,128)} %get-tuple-element.79), calls=%async_computation.1 | async-start | bytes 262144 | tf_op jit(solution)/shard_map/all_to_all | solution.py:840
  46.8 12.1 %all-to-all-start.2 = ((f32[32,8,128]{2,1,0:T(8,128)}), f32[32,8,128]{2,1,0:T(8,128)S(1)}, u32[]{:S(2)}, u32[]{:S(2)}) async-start(f32[32,8,128]{2,1,0:T(8,128)} %get-tuple-element.87), calls=%async_computation.2 | async-start | bytes 262144 | tf_op jit(solution)/shard_map/all_to_all | solution.py:840
  55.7 9.5 %collective-permute-start.9 = (f32[616,128]{1,0:T(8,128)}, f32[616,128]{1,0:T(8,128)S(1)}, u32[]{:S(2)}, u32[]{:S(2)}) collective-permute-start(f32[616,128]{1,0:T(8,128)} %get-tuple-element.93), channel_id=1, source_target_pairs={{0,4},{4,0},{8,12},{12,8},{16,20},{20,16},{24,28},{28,24},{1,5},{5... | collective-permute-start | bytes 946184 | tf_op jit(solution)/shard_map/ppermute | solution.py:850
  63.8 2.6 %collective-permute-start.8 = (f32[584,128]{1,0:T(8,128)S(1)}, f32[584,128]{1,0:T(8,128)S(1)}, u32[]{:S(2)}, u32[]{:S(2)}) collective-permute-start(f32[584,128]{1,0:T(8,128)S(1)} %get-tuple-element.91), channel_id=1, source_target_pairs={{0,4},{4,0},{8,12},{12,8},{16,20},{20,16},{24,28},{28,24},{1,5},{5... | collective-permute-start | bytes 897032 | tf_op jit(solution)/shard_map/ppermute | solution.py:850
  67.5 4.0 %collective-permute-start.10 = (f32[8,128]{1,0:T(8,128)S(1)}, f32[8,128]{1,0:T(8,128)S(1)}, u32[]{:S(2)}, u32[]{:S(2)}) collective-permute-start(f32[8,128]{1,0:T(8,128)S(1)} %get-tuple-element.94), channel_id=1, source_target_pairs={{0,4},{4,0},{8,12},{12,8},{16,20},{20,16},{24,28},{28,24},{1,5},{5... | collective-permute-start | bytes 12296 | tf_op jit(solution)/shard_map/ppermute | solution.py:850
  67.9 15.9 %all-to-all-start.3 = ((s16[16,88,128]{2,1,0:T(8,128)(2,1)}), s16[16,88,128]{2,1,0:T(8,128)(2,1)S(1)}, u32[]{:S(2)}, u32[]{:S(2)}) async-start(s16[16,88,128]{2,1,0:T(8,128)(2,1)} %get-tuple-element.97), calls=%async_computation.3 | async-start | bytes 720896 | tf_op jit(solution)/shard_map/all_to_all | solution.py:846
  77.1 5.0 %collective-permute-start.11 = (f32[16,128]{1,0:T(8,128)S(1)}, f32[16,128]{1,0:T(8,128)S(1)}, u32[]{:S(2)}, u32[]{:S(2)}) collective-permute-start(f32[16,128]{1,0:T(8,128)S(1)} %get-tuple-element.95.refs_4_.refs_1_), channel_id=1, source_target_pairs={{0,4},{4,0},{8,12},{12,8},{16,20},{20,16},{24,28},{28,24},{1,5},{5... | collective-permute-start | bytes 24584 | tf_op jit(solution)/shard_map/ppermute | solution.py:850
  82.0 22.9 %copy-start = (bf16[16,8,32,128]{3,2,1,0:T(8,128)(2,1)S(1)}, bf16[16,8,32,128]{3,2,1,0:T(8,128)(2,1)}, u32[]{:S(2)}) copy-start(bf16[16,8,32,128]{3,2,1,0:T(8,128)(2,1)} %refs_3_.1) | copy-start | bytes 3145732
  82.0 22.9 %copy-start.1 = (bf16[16,4096]{1,0:T(8,128)(2,1)S(1)}, bf16[16,4096]{1,0:T(8,128)(2,1)}, u32[]{:S(2)}) copy-start(bf16[16,4096]{1,0:T(8,128)(2,1)} %refs_11_.3) | copy-start | bytes 393220
  82.0 22.9 %copy-start.4 = (bf16[128]{0:T(256)(128)(2,1)S(1)}, bf16[128]{0:T(256)(128)(2,1)}, u32[]{:S(2)}) copy-start(bf16[128]{0:T(256)(128)(2,1)} %param.20) | copy-start | bytes 772
  82.0 22.9 %copy-start.5 = (bf16[128]{0:T(256)(128)(2,1)S(1)}, bf16[128]{0:T(256)(128)(2,1)}, u32[]{:S(2)}) copy-start(bf16[128]{0:T(256)(128)(2,1)} %param.24) | copy-start | bytes 772
  82.0 22.9 %copy-start.6 = (bf16[128]{0:T(256)(128)(2,1)S(1)}, bf16[128]{0:T(256)(128)(2,1)}, u32[]{:S(2)}) copy-start(bf16[128]{0:T(256)(128)(2,1)} %param.25) | copy-start | bytes 772
  82.0 22.9 %copy-start.7 = (f32[2,16,128]{2,1,0:T(8,128)S(1)}, f32[2,16,128]{2,1,0:T(8,128)}, u32[]{:S(2)}) copy-start(f32[2,16,128]{2,1,0:T(8,128)} %get-tuple-element.75.refs_3_.refs_5_) | copy-start | bytes 49156
  82.0 22.9 %copy-start.8 = (bf16[32,8,16,128]{3,2,1,0:T(8,128)(2,1)S(1)}, bf16[32,8,16,128]{3,2,1,0:T(8,128)(2,1)}, u32[]{:S(2)}) copy-start(bf16[32,8,16,128]{3,2,1,0:T(8,128)(2,1)} %get-tuple-element.62.refs_0_.refs_1_.refs_2_) | copy-start | bytes 3145732
  82.0 22.9 %copy-start.10 = (f32[16,256]{1,0:T(8,128)S(1)}, f32[16,256]{1,0:T(8,128)}, u32[]{:S(2)}) copy-start(f32[16,256]{1,0:T(8,128)} %get-tuple-element.80.refs_5_.refs_7_.refs_9_) | copy-start | bytes 49156
  82.1 22.9 %copy-start.11 = (bf16[16,512]{1,0:T(8,128)(2,1)S(1)}, bf16[16,512]{1,0:T(8,128)(2,1)}, u32[]{:S(2)}) copy-start(bf16[16,512]{1,0:T(8,128)(2,1)} %get-tuple-element.98.refs_10_) | copy-start | bytes 49156
  83.8 21.1 %copy-start.9 = (f32[32,8,16,128]{3,2,1,0:T(8,128)S(1)}, f32[32,8,16,128]{3,2,1,0:T(8,128)}, u32[]{:S(2)}) copy-start(f32[32,8,16,128]{3,2,1,0:T(8,128)} %get-tuple-element.96.refs_1_) | copy-start | bytes 6291460
  103.4 6.0 %collective-permute-start.12 = (bf16[16,104,128]{2,1,0:T(8,128)(2,1)S(1)}, bf16[16,104,128]{2,1,0:T(8,128)(2,1)S(1)}, u32[]{:S(2)}, u32[]{:S(2)}) collective-permute-start(bf16[16,104,128]{2,1,0:T(8,128)(2,1)S(1)} %all_to_all.25.refs_4_.refs_0_), channel_id=1, source_target_pairs={{0,4},{4,0},{8,12},{12,8},{16,20},{20,16},{24,28},{28,24},{1,5},{5... | collective-permute-start | bytes 1277960 | tf_op jit(solution)/shard_map/ppermute | solution.py:850
where the time goes:
time: 111 us
  Pallas kernels  48.4 us (44%)
  starting transfers between devices  32.2 us (29%)
  blocking collectives  18.6 us (17%)
  waiting for transfers between devices  9.59 us (9%)
  between operations  1.2 us (1%)
    pallas_call x15, Pallas kernels, kernel_call(): pl.pallas_call(run, out_shape=(*(pltpu.HBM(out.shape, out.dtype) for out...  48.4 us
    all_to_all x1, blocking collectives, to_chips(): return lax.all_to_all(payload, AXES, 0, 0, axis_index_groups=groups)  18.6 us
    all_to_all x3, starting transfers between devices, to_all(): return lax.all_to_all(payload, AXES, 0, 0)  15 us
    all_to_all x3, waiting for transfers between devices, to_all(): return lax.all_to_all(payload, AXES, 0, 0)  6.59 us
    ppermute x4, starting transfers between devices, pair_exchange(): return (one, lax.ppermute(other, axis, pairs))  5.08 us
    ppermute x4, starting transfers between devices, pair_exchange(): one = lax.ppermute(one, axis, [(i, i ^ 1) for i in range(count)])  4.73 us
    ppermute x5, starting transfers between devices, to_sibling(): lax.ppermute(payload, 'ha', [(i, i ^ 1) for i in range(lax.axis_size('ha'...  3.87 us
    all_to_all x1, starting transfers between devices, to_chips(): return lax.all_to_all(payload, AXES, 0, 0, axis_index_groups=groups)  3.55 us
  transfers between devices with their start and end apart: 17, of which 5 were waited for; matrix products, arithmetic and copies ran while one was open for 1% of the time, Pallas kernels for 34%

commit v1 on v0

--- a/solution.py
+++ b/solution.py
@@ -557,7 +557,7 @@
 
 def middle_grad(
     mid_far, pre_far, act_far, keep_two_far, gathered_ref, stat_ref, gain_ref, film_ref,
-    low_far, keep_ref, send_ref, two_ref,
+    low_far, keep_ref, send_ref, two_ref, bias_ref,
     mid_ref, pre_ref, act_ref, low_ref, mover,
 ):
     wide, tall, images, chans = mid_ref.shape
@@ -601,10 +601,11 @@
     at = 9 * (chans // 2)
     for ref in (keep_ref, send_ref):
         ref[at:] = jnp.broadcast_to(jnp.sum(kbias, axis=0, keepdims=True), (ref.shape[0] - at, chans))
+    bias_ref[...] = kbias
 
 
 def back_one(
-    low_far, xt_far, kernel_far, stat_ref, gain_ref, bias_ref, grad_far, pay_ref, low_ref, xt_ref, kernel_ref, out_ref, pair_ref, mover
+    low_far, xt_far, kernel_far, stat_ref, gain_ref, bias_ref, gbias_ref, lbias_ref, grad_far, pay_ref, low_ref, xt_ref, kernel_ref, out_ref, pair_ref, mover
 ):
     cols, rows, images, chans = xt_ref.shape
     loads = [mover.start(f, n) for f, n in ((kernel_far, kernel_ref), (low_far, low_ref), (xt_far, xt_ref))]
@@ -634,8 +635,8 @@
     plain, cross = state
     half = images // 2
     pay_ref[0:half] = pack_pair(group_total(plain * gain), group_total(cross * gain))
-    rest = [jnp.sum(v, axis=0, keepdims=True) for v in (cross, plain)]
-    short = pay_ref.shape[0] - half - 2
+    rest = [jnp.sum(v, axis=0, keepdims=True) for v in (cross, plain, gbias_ref[...], lbias_ref[...])]
+    short = pay_ref.shape[0] - half - 4
     pay_ref[half:] = jnp.concatenate(rest + [jnp.zeros((short, chans), F32)], axis=0)
 
 
@@ -675,7 +676,8 @@
     one_ref[...] = keep_one_ref[...] + came_one_ref[...]
     two_ref[...] = keep_two_ref[...] + came_two_ref[...]
     extra_ref[0:extras_two] = two_ref[taps : taps + extras_two]
-    extra_ref[extras_two : extras_two + extras_one] = one_ref[taps : taps + extras_one]
+    if extras_one:
+        extra_ref[extras_two : extras_two + extras_one] = one_ref[taps : taps + extras_one]
     token_ref[...] = extra_ref[0:8]
     powers = []
     for ref, count in ((one_ref, taps), (two_ref, taps), (extra_ref, extra_ref.shape[0])):
@@ -791,10 +793,8 @@
     sums = sums_of(own_ref, start + 2 * more, whole)
     vec_refs[0][...] = jnp.sum(scale * cross, axis=0, keepdims=True)
     vec_refs[1][...] = jnp.sum(scale * plain, axis=0, keepdims=True)
-    for at, row in enumerate((extra_ref[2 * images : 2 * images + 1], extra_ref[2 * images + 1 : 2 * images + 2])):
-        vec_refs[2 + at][...] = row
-    vec_refs[4][...] = sums[whole - 2 : whole - 1]
-    vec_refs[5][...] = sums[whole - 1 : whole]
+    for at, row in ((4, whole - 4), (5, whole - 3), (2, whole - 2), (3, whole - 1)):
+        vec_refs[at][...] = sums[row : row + 1]
     terms = three_terms(film_grad)
     ints = ints_ref.shape[1]
 
@@ -947,8 +947,8 @@
 
     taps = 9 * (chans // 2)
     share = -(-taps // chips)
-    extras_two = 2 * images + 1
-    extras_one = 1
+    extras_two = 2 * images
+    extras_one = 0
     halves_two = shaped((taps + 2 * images + 8, chans), F32)
     halves_one = shaped((taps + 8, chans), F32)
     keep_two, send_two = kernel_call(
@@ -956,9 +956,9 @@
         scratch=buffers(act_two, gt, halves_two, halves_two), sems=4, cost=3.0,
     )
     came_two = to_sibling(send_two)
-    low, keep_one, send_one, keep_two = kernel_call(
+    low, keep_one, send_one, keep_two, kbias_one_local = kernel_call(
         middle_grad, far=(mid, pre_two_grad, act_one, keep_two), near=(moments_three,), tiny=(stat_two, gain_two, film),
-        far_out=(rim,), near_out=(halves_one, halves_one, halves_two),
+        far_out=(rim,), near_out=(halves_one, halves_one, halves_two), tiny_out=(per_image,),
         scratch=buffers(mid, pre_two_grad, act_one, rim), sems=24, cost=6.0,
     )
     came_one = to_sibling(send_one)
@@ -972,9 +972,9 @@
         sems=3, cost=1.0,
     )
     gathered = to_chips(terms)
-    whole = half + 2
+    whole = half + 4
     norm_one_grad, pay_four = kernel_call(
-        back_one, far=(low, xt, conv_one), tiny=(stat_one, gain_one, bias_one), far_out=(block_wide,),
+        back_one, far=(low, xt, conv_one), tiny=(stat_one, gain_one, bias_one, kbias_two_local, kbias_one_local), far_out=(block_wide,),
         near_out=(shaped((2 * half, chans), F32),),
         scratch=buffers(rim, block, conv_one, block_wide) + (pair_back,), sems=16, cost=5.0,
         after_near=(to_sibling(token),),

time: 111 us -> 111 us (level)
  no operation moved by 1% of the time
where the time goes in v1:
time: 111 us
  Pallas kernels  48.5 us (44%)
  starting transfers between devices  32.2 us (29%)
  blocking collectives  19.3 us (17%)
  waiting for transfers between devices  8.84 us (8%)
  between operations  1.2 us (1%)
    pallas_call x15, Pallas kernels, kernel_call(): pl.pallas_call(run, out_shape=(*(pltpu.HBM(out.shape, out.dtype) for out...  48.5 us
    all_to_all x1, blocking collectives, to_chips(): return lax.all_to_all(payload, AXES, 0, 0, axis_index_groups=groups)  19.3 us
    all_to_all x3, starting transfers between devices, to_all(): return lax.all_to_all(payload, AXES, 0, 0)  15 us
    all_to_all x3, waiting for transfers between devices, to_all(): return lax.all_to_all(payload, AXES, 0, 0)  6.59 us
    ppermute x4, starting transfers between devices, pair_exchange(): return (one, lax.ppermute(other, axis, pairs))  5.08 us
    ppermute x4, starting transfers between devices, pair_exchange(): one = lax.ppermute(one, axis, [(i, i ^ 1) for i in range(count)])  4.73 us
    ppermute x5, starting transfers between devices, to_sibling(): lax.ppermute(payload, 'ha', [(i, i ^ 1) for i in range(lax.axis_size('ha'...  3.85 us
    all_to_all x1, starting transfers between devices, to_chips(): return lax.all_to_all(payload, AXES, 0, 0, axis_index_groups=groups)  3.54 us
  transfers between devices with their start and end apart: 17, of which 5 were waited for; matrix products, arithmetic and copies ran while one was open for 1% of the time, Pallas kernels for 34%

profile of v1, /device:TPU:1, one launch (start us, length us, event | category | flops | bytes accessed | tf_op | source)
XLA Modules:
  0.0 110.7 jit_solution(12332857458083925174)
XLA Ops:
  0.6 2.7 %prepare_x.1 = (bf16[32,8,16,128]{3,2,1,0:T(8,128)(2,1)}, bf16[32,2,16,128]{3,2,1,0:T(8,128)(2,1)S(1)}, bf16[32,2,16,128]{3,2,1,0:T(8,128)(2,1)S(1)}, bf16[4,8,16,128]{3,2,1,0:T(8,128)(2,1)S(1)}, f32[8,128]{1,0:T(8,128)S(1)}) custom-call(bf16[16,8,32,128]{3,2,1,0:T(8,128)(2,1)} %refs_0_.3), custom_call_target="tpu_custom_call" | custom-call | flops 2529999872 | tf_op jit(solution)/shard_map/prepare_x/pallas_call | solution.py:57
  3.5 2.6 %collective-permute-start.1 = (bf16[32,2,16,128]{3,2,1,0:T(8,128)(2,1)S(1)}, bf16[32,2,16,128]{3,2,1,0:T(8,128)(2,1)S(1)}, u32[]{:S(2)}, u32[]{:S(2)}) collective-permute-start(bf16[32,2,16,128]{3,2,1,0:T(8,128)(2,1)S(1)} %get-tuple-element.65), channel_id=1, source_target_pairs={{0,28},{4,8},{8,4},{12,16},{16,12},{20,24},{24,20},{28,0},{1,29},{... | collective-permute-start | bytes 786440 | tf_op jit(solution)/shard_map/ppermute | solution.py:859
  6.1 2.6 %prepare_g.1 = (bf16[32,8,16,128]{3,2,1,0:T(8,128)(2,1)}, f32[32,8,128]{2,1,0:T(8,128)}, bf16[32,2,16,128]{3,2,1,0:T(8,128)(2,1)S(1)}, bf16[32,2,16,128]{3,2,1,0...) custom-call(bf16[16,8,32,128]{3,2,1,0:T(8,128)(2,1)} %refs_3_.1, ...), custom_call_target="tpu_custom_call" | custom-call | flops 2200000000 | tf_op jit(solution)/shard_map/prepare_g/pallas_call | solution.py:57
  8.7 5.1 %all-to-all-start = ((f32[32,8,128]{2,1,0:T(8,128)}), f32[32,8,128]{2,1,0:T(8,128)S(1)}, u32[]{:S(2)}, u32[]{:S(2)}) async-start(f32[32,8,128]{2,1,0:T(8,128)} %get-tuple-element.70), calls=%async_computation | async-start | bytes 262144 | tf_op jit(solution)/shard_map/all_to_all | solution.py:840
  13.9 1.5 %collective-permute-start.2 = (bf16[2,12,16,128]{3,2,1,0:T(8,128)(2,1)S(1)}, bf16[2,12,16,128]{3,2,1,0:T(8,128)(2,1)S(1)}, u32[]{:S(2)}, u32[]{:S(2)}) collective-permute-start(bf16[2,12,16,128]{3,2,1,0:T(8,128)(2,1)S(1)} %get-tuple-element.67), channel_id=1, source_target_pairs={{0,1},{1,0},{2,3},{3,2},{4,5},{5,4},{6,7},{7,6},{8,9},{9,8},{10,11... | collective-permute-start | bytes 294920 | tf_op jit(solution)/shard_map/ppermute | solution.py:858
  15.3 0.7 collective-permute-start.3
  16.0 0.7 collective-permute-start.4
  16.7 1.1 %collective-permute-start.5 = (bf16[32,2,16,128]{3,2,1,0:T(8,128)(2,1)S(1)}, bf16[32,2,16,128]{3,2,1,0:T(8,128)(2,1)S(1)}, u32[]{:S(2)}, u32[]{:S(2)}) collective-permute-start(bf16[32,2,16,128]{3,2,1,0:T(8,128)(2,1)S(1)} %get-tuple-element.74), channel_id=1, source_target_pairs={{0,28},{4,8},{8,4},{12,16},{16,12},{20,24},{24,20},{28,0},{1,29},{... | collective-permute-start | bytes 786440 | tf_op jit(solution)/shard_map/ppermute | solution.py:859
  18.4 2.7 %all-to-all-done.refs_6_ = f32[32,8,128]{2,1,0:T(8,128)S(1)} async-done(((f32[32,8,128]{2,1,0:T(8,128)}), f32[32,8,128]{2,1,0:T(8,128)S(1)}, u32[]{:S(2)}, u32[]{:S(2)}) %all-to-all-start) | async-done | bytes 131104 | tf_op jit(solution)/shard_map/all_to_all | solution.py:840
  21.1 5.6 %first_half.1 = (bf16[36,12,16,128]{3,2,1,0:T(8,128)(2,1)}, f32[34,10,16,128]{3,2,1,0:T(8,128)}, f32[32,8,128]{2,1,0:T(8,128)}, f32[2,16,128]{2,1,0:T(8,128)}) custom-call(bf16[32,8,16,128]{3,2,1,0:T(8,128)(2,1)} %get-tuple-element.63.refs_0_.refs_1_.refs_2_, bf16[3,3,128,128]{3,2,1,0:T(8,128)(2,1)} %refs_2_.3, ...), custom_call_target="tpu_custom_call" | custom-call | flops 6049999872 | tf_op jit(solution)/shard_map/first_half/pallas_call | solution.py:57
  26.8 2.5 %collective-permute-start.6 = (bf16[2,12,16,128]{3,2,1,0:T(8,128)(2,1)S(1)}, bf16[2,12,16,128]{3,2,1,0:T(8,128)(2,1)S(1)}, u32[]{:S(2)}, u32[]{:S(2)}) collective-permute-start(bf16[2,12,16,128]{3,2,1,0:T(8,128)(2,1)S(1)} %get-tuple-element.77), channel_id=1, source_target_pairs={{0,1},{1,0},{2,3},{3,2},{4,5},{5,4},{6,7},{7,6},{8,9},{9,8},{10,11... | collective-permute-start | bytes 294920 | tf_op jit(solution)/shard_map/ppermute | solution.py:858
  29.2 0.7 collective-permute-start.7
  29.9 5.2 %all-to-all-start.1 = ((f32[32,8,128]{2,1,0:T(8,128)}), f32[32,8,128]{2,1,0:T(8,128)S(1)}, u32[]{:S(2)}, u32[]{:S(2)}) async-start(f32[32,8,128]{2,1,0:T(8,128)} %get-tuple-element.80), calls=%async_computation.1 | async-start | bytes 262144 | tf_op jit(solution)/shard_map/all_to_all | solution.py:840
  35.1 6.1 %back_two.1 = (f32[34,10,16,128]{3,2,1,0:T(8,128)}, f32[16,256]{1,0:T(8,128)}, bf16[16,512]{1,0:T(8,128)(2,1)}) custom-call(bf16[32,8,16,128]{3,2,1,0:T(8,128)(2,1)} %get-tuple-element.72.refs_0_.refs_1_, bf16[3,3,128,128]{3,2,1,0:T(8,128)(2,1)} %refs_1_.5, bf16[4608,256]{1,0:T(8,128)(2,1)} %refs_0_.5, ...), custom_call_target="tpu_custom_call" | custom-call | flops 5500000256 | tf_op jit(solution)/shard_map/back_two/pallas_call | solution.py:57
  41.3 1.1 %all-to-all-done.1.refs_2_ = f32[32,8,128]{2,1,0:T(8,128)S(1)} async-done(((f32[32,8,128]{2,1,0:T(8,128)}), f32[32,8,128]{2,1,0:T(8,128)S(1)}, u32[]{:S(2)}, u32[]{:S(2)}) %all-to-all-start.1) | async-done | bytes 131104 | tf_op jit(solution)/shard_map/all_to_all | solution.py:840
  42.4 4.4 %second_norm.1 = (bf16[34,10,16,128]{3,2,1,0:T(8,128)(2,1)}, bf16[34,10,16,128]{3,2,1,0:T(8,128)(2,1)}, f32[32,8,128]{2,1,0:T(8,128)}, f32[2,16,128]{2,1,0:T(8,128)}, f32[2,16,128]{2,1,0:T(8,128)}) custom-call(f32[34,10,16,128]{3,2,1,0:T(8,128)} %get-tuple-element.71.refs_0_, f32[34,10,16,128]{3,2,1,0:T(8,128)} %get-tuple-element.79.refs_1_, ...), custom_call_target="tpu_custom_call" | custom-call | flops 3520000000 | tf_op jit(solution)/shard_map/second_norm/pallas_call | solution.py:57
  46.8 4.7 %all-to-all-start.2 = ((f32[32,8,128]{2,1,0:T(8,128)}), f32[32,8,128]{2,1,0:T(8,128)S(1)}, u32[]{:S(2)}, u32[]{:S(2)}) async-start(f32[32,8,128]{2,1,0:T(8,128)} %get-tuple-element.88), calls=%async_computation.2 | async-start | bytes 262144 | tf_op jit(solution)/shard_map/all_to_all | solution.py:840
  51.5 4.2 %kernel_two.1 = (f32[616,128]{1,0:T(8,128)}, f32[616,128]{1,0:T(8,128)}) custom-call(bf16[34,10,16,128]{3,2,1,0:T(8,128)(2,1)} %get-tuple-element.82.refs_0_, bf16[32,8,16,128]{3,2,1,0:T(8,128)(2,1)} %get-tuple-element.72.refs_0_.refs_1_, f32[2,16,128]{2,1,0:T(8,128)} %get-tuple-element.85.refs_2_, f32[16,128]{1,0:T(8,128)} %get-tuple-element.86.refs_3_.refs_6_), custom_call_target="tpu_custom_call" | custom-call | flops 3300000000 | tf_op jit(solution)/shard_map/kernel_two/pallas_call | solution.py:57
  56.1 2.8 %all-to-all-done.2.refs_4_ = f32[32,8,128]{2,1,0:T(8,128)S(1)} async-done(((f32[32,8,128]{2,1,0:T(8,128)}), f32[32,8,128]{2,1,0:T(8,128)S(1)}, u32[]{:S(2)}, u32[]{:S(2)}) %all-to-all-start.2) | async-done | bytes 131104 | tf_op jit(solution)/shard_map/all_to_all | solution.py:840
  58.8 4.9 %middle_grad.1 = (bf16[34,10,16,128]{3,2,1,0:T(8,128)(2,1)}, f32[584,128]{1,0:T(8,128)S(1)}, f32[584,128]{1,0:T(8,128)S(1)}, f32[616,128]{1,0:T(8,128)S(1)}, f32[16,128]{1,0:T(8,128)}) custom-call(f32[34,10,16,128]{3,2,1,0:T(8,128)} %get-tuple-element.71.refs_0_, bf16[34,10,16,128]{3,2,1,0:T(8,128)(2,1)} %get-tuple-element.83.refs_1_, ...), custom_call_target="tpu_custom_call" | custom-call | flops 6600000000 | tf_op jit(solution)/shard_map/middle_grad/pallas_call | solution.py:57
  63.8 1.4 %collective-permute-start.8 = (f32[584,128]{1,0:T(8,128)S(1)}, f32[584,128]{1,0:T(8,128)S(1)}, u32[]{:S(2)}, u32[]{:S(2)}) collective-permute-start(f32[584,128]{1,0:T(8,128)S(1)} %get-tuple-element.93), channel_id=1, source_target_pairs={{0,4},{4,0},{8,12},{12,8},{16,20},{20,16},{24,28},{28,24},{1,5},{5... | collective-permute-start | bytes 897032 | tf_op jit(solution)/shard_map/ppermute | solution.py:850
  65.2 1.2 %collective-permute-done.8.refs_1_ = f32[584,128]{1,0:T(8,128)S(1)} collective-permute-done((f32[584,128]{1,0:T(8,128)S(1)}, f32[584,128]{1,0:T(8,128)S(1)}, u32[]{:S(2)}, u32[]{:S(2)}) %collective-permute-start.8) | collective-permute-done | bytes 299040 | tf_op jit(solution)/shard_map/ppermute | solution.py:850
  66.4 1.1 pack_terms.1
  67.9 3.5 %all-to-all-start.3 = ((s16[16,80,128]{2,1,0:T(8,128)(2,1)}), s16[16,80,128]{2,1,0:T(8,128)(2,1)S(1)}, u32[]{:S(2)}, u32[]{:S(2)}) async-start(s16[16,80,128]{2,1,0:T(8,128)(2,1)} %get-tuple-element.99), calls=%async_computation.3 | async-start | bytes 655360 | tf_op jit(solution)/shard_map/all_to_all | solution.py:846
  71.5 5.6 %back_one.1 = (f32[32,8,16,128]{3,2,1,0:T(8,128)}, f32[16,128]{1,0:T(8,128)S(1)}) custom-call(bf16[34,10,16,128]{3,2,1,0:T(8,128)(2,1)} %get-tuple-element.90.refs_0_, bf16[32,8,16,128]{3,2,1,0:T(8,128)(2,1)} %get-tuple-element.63.refs_0_.refs_1_.refs_2_, bf16[3,3,128,128]{3,2,1,0:T(8,128)(2,1)} %refs_2_.3, f32[2,16,128]{2,1,0:T(8,128)} %get-tuple-element.76.refs_3_.refs_5_, ...), custom_call_target="tpu_custom_call" | custom-call | flops 5500000256 | tf_op jit(solution)/shard_map/back_one/pallas_call | solution.py:57
  77.3 4.7 %mix.1.refs_3_ = bf16[16,8,32,128]{3,2,1,0:T(8,128)(2,1)} custom-call(bf16[34,10,16,128]{3,2,1,0:T(8,128)(2,1)} %get-tuple-element.82.refs_0_, bf16[3,3,128,128]{3,2,1,0:T(8,128)(2,1)} %refs_1_.5, bf16[32,8,16,128]{3,2,1,0:T(8,128)(2,1)} %get-tuple-element.63.refs_0_.refs_1_.refs_2_, bf16[1,128]{1,0:T(2,128)(2,1)} %bitcast.26, ...), custom_call_target="tpu_custom_call" | custom-call | flops 3960000000 | tf_op jit(solution)/shard_map/mix/pallas_call | solution.py:57
  82.1 1.0 all-to-all-done.3.refs_0_
  83.1 1.0 add_terms.1
  84.1 19.3 %all_to_all.25.refs_4_.refs_0_ = bf16[16,104,128]{2,1,0:T(8,128)(2,1)S(1)} all-to-all(bf16[16,104,128]{2,1,0:T(8,128)(2,1)} %add_terms.1), channel_id=1, replica_groups={{0,1,2,3,8,9,10,11,16,17,18,19,24,25,26,27},{4,5,6,7,12,13,14,15,20,21,..., dimensions={0} | all-to-all | bytes 851968 | tf_op jit(solution)/shard_map/all_to_all | solution.py:846
  103.4 1.5 %collective-permute-start.12 = (bf16[16,104,128]{2,1,0:T(8,128)(2,1)S(1)}, bf16[16,104,128]{2,1,0:T(8,128)(2,1)S(1)}, u32[]{:S(2)}, u32[]{:S(2)}) collective-permute-start(bf16[16,104,128]{2,1,0:T(8,128)(2,1)S(1)} %all_to_all.25.refs_4_.refs_0_), channel_id=1, source_target_pairs={{0,4},{4,0},{8,12},{12,8},{16,20},{20,16},{24,28},{28,24},{1,5},{5... | collective-permute-start | bytes 1277960 | tf_op jit(solution)/shard_map/ppermute | solution.py:850
  105.0 4.4 %last_grads.1 = (bf16[16,8,32,128]{3,2,1,0:T(8,128)(2,1)}, f32[4608,256]{1,0:T(8,128)}, f32[16,4096]{1,0:T(8,128)}, f32[1,256]{1,0:T(1,128)}, f32[1,128]{1,0:T(1...) custom-call(bf16[4608,256]{1,0:T(8,128)(2,1)} %refs_0_.5, ...), custom_call_target="tpu_custom_call" | custom-call | flops 6600000000 | tf_op jit(solution)/shard_map/last_grads/pallas_call | solution.py:57
  109.4 1.1 %spread_out.1 = (f32[9,128,128]{2,1,0:T(8,128)}, f32[9,128,128]{2,1,0:T(8,128)}) custom-call(bf16[16,104,128]{2,1,0:T(8,128)(2,1)S(1)} %all_to_all.25.refs_4_.refs_0_, bf16[16,104,128]{2,1,0:T(8,128)(2,1)S(1)} %collective-permute-done.12.refs_1_, bf16[16,8,32,128]{3,2,1,0:T(8,128)(2,1)} %get-tuple-element.51.refs_2_), custom_call_target="tpu_custom_call" | custom-call | flops 2200000000 | tf_op jit(solution)/shard_map/spread_out/pallas_call | solution.py:57
  (45 shorter events, 1.9 us)
Async XLA Ops:
  3.4 10.4 %collective-permute-start = (bf16[32,2,16,128]{3,2,1,0:T(8,128)(2,1)S(1)}, bf16[32,2,16,128]{3,2,1,0:T(8,128)(2,1)S(1)}, u32[]{:S(2)}, u32[]{:S(2)}) collective-permute-start(bf16[32,2,16,128]{3,2,1,0:T(8,128)(2,1)S(1)} %get-tuple-element.64), channel_id=1, source_target_pairs={{0,4},{4,0},{8,12},{12,8},{16,20},{20,16},{24,28},{28,24},{1,5},{5... | collective-permute-start | bytes 786440 | tf_op jit(solution)/shard_map/ppermute | solution.py:858
  3.5 10.3 %collective-permute-start.1 = (bf16[32,2,16,128]{3,2,1,0:T(8,128)(2,1)S(1)}, bf16[32,2,16,128]{3,2,1,0:T(8,128)(2,1)S(1)}, u32[]{:S(2)}, u32[]{:S(2)}) collective-permute-start(bf16[32,2,16,128]{3,2,1,0:T(8,128)(2,1)S(1)} %get-tuple-element.65), channel_id=1, source_target_pairs={{0,28},{4,8},{8,4},{12,16},{16,12},{20,24},{24,20},{28,0},{1,29},{... | collective-permute-start | bytes 786440 | tf_op jit(solution)/shard_map/ppermute | solution.py:859
  6.1 11.7 %copy-start.12 = (bf16[256]{0:T(256)(128)(2,1)S(1)}, bf16[256]{0:T(256)(128)(2,1)}, u32[]{:S(2)}) copy-start(bf16[256]{0:T(256)(128)(2,1)} %param.27) | copy-start | bytes 1540
  8.7 12.4 %all-to-all-start = ((f32[32,8,128]{2,1,0:T(8,128)}), f32[32,8,128]{2,1,0:T(8,128)S(1)}, u32[]{:S(2)}, u32[]{:S(2)}) async-start(f32[32,8,128]{2,1,0:T(8,128)} %get-tuple-element.70), calls=%async_computation | async-start | bytes 262144 | tf_op jit(solution)/shard_map/all_to_all | solution.py:840
  13.9 7.2 %collective-permute-start.2 = (bf16[2,12,16,128]{3,2,1,0:T(8,128)(2,1)S(1)}, bf16[2,12,16,128]{3,2,1,0:T(8,128)(2,1)S(1)}, u32[]{:S(2)}, u32[]{:S(2)}) collective-permute-start(bf16[2,12,16,128]{3,2,1,0:T(8,128)(2,1)S(1)} %get-tuple-element.67), channel_id=1, source_target_pairs={{0,1},{1,0},{2,3},{3,2},{4,5},{5,4},{6,7},{7,6},{8,9},{9,8},{10,11... | collective-permute-start | bytes 294920 | tf_op jit(solution)/shard_map/ppermute | solution.py:858
  15.3 5.8 %collective-permute-start.3 = (bf16[2,12,16,128]{3,2,1,0:T(8,128)(2,1)S(1)}, bf16[2,12,16,128]{3,2,1,0:T(8,128)(2,1)S(1)}, u32[]{:S(2)}, u32[]{:S(2)}) collective-permute-start(bf16[2,12,16,128]{3,2,1,0:T(8,128)(2,1)S(1)} %get-tuple-element.68), channel_id=1, source_target_pairs={{0,0},{1,2},{2,1},{3,3},{4,4},{5,6},{6,5},{7,7},{8,8},{9,10},{10,9... | collective-permute-start | bytes 294920 | tf_op jit(solution)/shard_map/ppermute | solution.py:859
  16.0 10.7 %collective-permute-start.4 = (bf16[32,2,16,128]{3,2,1,0:T(8,128)(2,1)S(1)}, bf16[32,2,16,128]{3,2,1,0:T(8,128)(2,1)S(1)}, u32[]{:S(2)}, u32[]{:S(2)}) collective-permute-start(bf16[32,2,16,128]{3,2,1,0:T(8,128)(2,1)S(1)} %get-tuple-element.73), channel_id=1, source_target_pairs={{0,4},{4,0},{8,12},{12,8},{16,20},{20,16},{24,28},{28,24},{1,5},{5... | collective-permute-start | bytes 786440 | tf_op jit(solution)/shard_map/ppermute | solution.py:858
  16.7 10.0 %collective-permute-start.5 = (bf16[32,2,16,128]{3,2,1,0:T(8,128)(2,1)S(1)}, bf16[32,2,16,128]{3,2,1,0:T(8,128)(2,1)S(1)}, u32[]{:S(2)}, u32[]{:S(2)}) collective-permute-start(bf16[32,2,16,128]{3,2,1,0:T(8,128)(2,1)S(1)} %get-tuple-element.74), channel_id=1, source_target_pairs={{0,28},{4,8},{8,4},{12,16},{16,12},{20,24},{24,20},{28,0},{1,29},{... | collective-permute-start | bytes 786440 | tf_op jit(solution)/shard_map/ppermute | solution.py:859
  21.1 14.0 %copy-start.2 = (s32[16]{0:T(128)S(1)}, s32[16]{0:T(128)}, u32[]{:S(2)}) copy-start(s32[16]{0:T(128)} %refs_10_.1) | copy-start | bytes 196
  21.1 14.0 %copy-start.3 = (s32[16]{0:T(128)S(1)}, s32[16]{0:T(128)}, u32[]{:S(2)}) copy-start(s32[16]{0:T(128)} %refs_11_.2) | copy-start | bytes 196
  26.8 8.3 %collective-permute-start.6 = (bf16[2,12,16,128]{3,2,1,0:T(8,128)(2,1)S(1)}, bf16[2,12,16,128]{3,2,1,0:T(8,128)(2,1)S(1)}, u32[]{:S(2)}, u32[]{:S(2)}) collective-permute-start(bf16[2,12,16,128]{3,2,1,0:T(8,128)(2,1)S(1)} %get-tuple-element.77), channel_id=1, source_target_pairs={{0,1},{1,0},{2,3},{3,2},{4,5},{5,4},{6,7},{7,6},{8,9},{9,8},{10,11... | collective-permute-start | bytes 294920 | tf_op jit(solution)/shard_map/ppermute | solution.py:858
  29.2 5.8 %collective-permute-start.7 = (bf16[2,12,16,128]{3,2,1,0:T(8,128)(2,1)S(1)}, bf16[2,12,16,128]{3,2,1,0:T(8,128)(2,1)S(1)}, u32[]{:S(2)}, u32[]{:S(2)}) collective-permute-start(bf16[2,12,16,128]{3,2,1,0:T(8,128)(2,1)S(1)} %get-tuple-element.78), channel_id=1, source_target_pairs={{0,0},{1,2},{2,1},{3,3},{4,4},{5,6},{6,5},{7,7},{8,8},{9,10},{10,9... | collective-permute-start | bytes 294920 | tf_op jit(solution)/shard_map/ppermute | solution.py:859
  29.9 12.5 %all-to-all-start.1 = ((f32[32,8,128]{2,1,0:T(8,128)}), f32[32,8,128]{2,1,0:T(8,128)S(1)}, u32[]{:S(2)}, u32[]{:S(2)}) async-start(f32[32,8,128]{2,1,0:T(8,128)} %get-tuple-element.80), calls=%async_computation.1 | async-start | bytes 262144 | tf_op jit(solution)/shard_map/all_to_all | solution.py:840
  46.8 12.1 %all-to-all-start.2 = ((f32[32,8,128]{2,1,0:T(8,128)}), f32[32,8,128]{2,1,0:T(8,128)S(1)}, u32[]{:S(2)}, u32[]{:S(2)}) async-start(f32[32,8,128]{2,1,0:T(8,128)} %get-tuple-element.88), calls=%async_computation.2 | async-start | bytes 262144 | tf_op jit(solution)/shard_map/all_to_all | solution.py:840
  55.7 9.5 %collective-permute-start.9 = (f32[616,128]{1,0:T(8,128)}, f32[616,128]{1,0:T(8,128)S(1)}, u32[]{:S(2)}, u32[]{:S(2)}) collective-permute-start(f32[616,128]{1,0:T(8,128)} %get-tuple-element.95), channel_id=1, source_target_pairs={{0,4},{4,0},{8,12},{12,8},{16,20},{20,16},{24,28},{28,24},{1,5},{5... | collective-permute-start | bytes 946184 | tf_op jit(solution)/shard_map/ppermute | solution.py:850
  63.8 2.6 %collective-permute-start.8 = (f32[584,128]{1,0:T(8,128)S(1)}, f32[584,128]{1,0:T(8,128)S(1)}, u32[]{:S(2)}, u32[]{:S(2)}) collective-permute-start(f32[584,128]{1,0:T(8,128)S(1)} %get-tuple-element.93), channel_id=1, source_target_pairs={{0,4},{4,0},{8,12},{12,8},{16,20},{20,16},{24,28},{28,24},{1,5},{5... | collective-permute-start | bytes 897032 | tf_op jit(solution)/shard_map/ppermute | solution.py:850
  67.5 4.0 %collective-permute-start.10 = (f32[8,128]{1,0:T(8,128)S(1)}, f32[8,128]{1,0:T(8,128)S(1)}, u32[]{:S(2)}, u32[]{:S(2)}) collective-permute-start(f32[8,128]{1,0:T(8,128)S(1)} %get-tuple-element.96), channel_id=1, source_target_pairs={{0,4},{4,0},{8,12},{12,8},{16,20},{20,16},{24,28},{28,24},{1,5},{5... | collective-permute-start | bytes 12296 | tf_op jit(solution)/shard_map/ppermute | solution.py:850
  67.9 15.2 %all-to-all-start.3 = ((s16[16,80,128]{2,1,0:T(8,128)(2,1)}), s16[16,80,128]{2,1,0:T(8,128)(2,1)S(1)}, u32[]{:S(2)}, u32[]{:S(2)}) async-start(s16[16,80,128]{2,1,0:T(8,128)(2,1)} %get-tuple-element.99), calls=%async_computation.3 | async-start | bytes 655360 | tf_op jit(solution)/shard_map/all_to_all | solution.py:846
  77.1 5.0 %collective-permute-start.11 = (f32[16,128]{1,0:T(8,128)S(1)}, f32[16,128]{1,0:T(8,128)S(1)}, u32[]{:S(2)}, u32[]{:S(2)}) collective-permute-start(f32[16,128]{1,0:T(8,128)S(1)} %get-tuple-element.97.refs_4_.refs_1_), channel_id=1, source_target_pairs={{0,4},{4,0},{8,12},{12,8},{16,20},{20,16},{24,28},{28,24},{1,5},{5... | collective-permute-start | bytes 24584 | tf_op jit(solution)/shard_map/ppermute | solution.py:850
  82.0 22.9 %copy-start = (bf16[16,8,32,128]{3,2,1,0:T(8,128)(2,1)S(1)}, bf16[16,8,32,128]{3,2,1,0:T(8,128)(2,1)}, u32[]{:S(2)}) copy-start(bf16[16,8,32,128]{3,2,1,0:T(8,128)(2,1)} %refs_3_.1) | copy-start | bytes 3145732
  82.0 22.9 %copy-start.1 = (bf16[16,4096]{1,0:T(8,128)(2,1)S(1)}, bf16[16,4096]{1,0:T(8,128)(2,1)}, u32[]{:S(2)}) copy-start(bf16[16,4096]{1,0:T(8,128)(2,1)} %refs_11_.3) | copy-start | bytes 393220
  82.0 22.9 %copy-start.4 = (bf16[128]{0:T(256)(128)(2,1)S(1)}, bf16[128]{0:T(256)(128)(2,1)}, u32[]{:S(2)}) copy-start(bf16[128]{0:T(256)(128)(2,1)} %param.20) | copy-start | bytes 772
  82.0 22.9 %copy-start.5 = (bf16[128]{0:T(256)(128)(2,1)S(1)}, bf16[128]{0:T(256)(128)(2,1)}, u32[]{:S(2)}) copy-start(bf16[128]{0:T(256)(128)(2,1)} %param.24) | copy-start | bytes 772
  82.1 22.9 %copy-start.6 = (bf16[128]{0:T(256)(128)(2,1)S(1)}, bf16[128]{0:T(256)(128)(2,1)}, u32[]{:S(2)}) copy-start(bf16[128]{0:T(256)(128)(2,1)} %param.25) | copy-start | bytes 772
  82.1 22.9 %copy-start.7 = (f32[2,16,128]{2,1,0:T(8,128)S(1)}, f32[2,16,128]{2,1,0:T(8,128)}, u32[]{:S(2)}) copy-start(f32[2,16,128]{2,1,0:T(8,128)} %get-tuple-element.76.refs_3_.refs_5_) | copy-start | bytes 49156
  82.1 22.9 %copy-start.8 = (bf16[32,8,16,128]{3,2,1,0:T(8,128)(2,1)S(1)}, bf16[32,8,16,128]{3,2,1,0:T(8,128)(2,1)}, u32[]{:S(2)}) copy-start(bf16[32,8,16,128]{3,2,1,0:T(8,128)(2,1)} %get-tuple-element.63.refs_0_.refs_1_.refs_2_) | copy-start | bytes 3145732
  82.1 22.9 %copy-start.10 = (f32[16,256]{1,0:T(8,128)S(1)}, f32[16,256]{1,0:T(8,128)}, u32[]{:S(2)}) copy-start(f32[16,256]{1,0:T(8,128)} %get-tuple-element.81.refs_5_.refs_7_.refs_9_) | copy-start | bytes 49156
  82.1 22.9 %copy-start.11 = (bf16[16,512]{1,0:T(8,128)(2,1)S(1)}, bf16[16,512]{1,0:T(8,128)(2,1)}, u32[]{:S(2)}) copy-start(bf16[16,512]{1,0:T(8,128)(2,1)} %get-tuple-element.100.refs_10_) | copy-start | bytes 49156
  83.1 21.8 %copy-start.9 = (f32[32,8,16,128]{3,2,1,0:T(8,128)S(1)}, f32[32,8,16,128]{3,2,1,0:T(8,128)}, u32[]{:S(2)}) copy-start(f32[32,8,16,128]{3,2,1,0:T(8,128)} %get-tuple-element.98.refs_1_) | copy-start | bytes 6291460
  103.4 6.0 %collective-permute-start.12 = (bf16[16,104,128]{2,1,0:T(8,128)(2,1)S(1)}, bf16[16,104,128]{2,1,0:T(8,128)(2,1)S(1)}, u32[]{:S(2)}, u32[]{:S(2)}) collective-permute-start(bf16[16,104,128]{2,1,0:T(8,128)(2,1)S(1)} %all_to_all.25.refs_4_.refs_0_), channel_id=1, source_target_pairs={{0,4},{4,0},{8,12},{12,8},{16,20},{20,16},{24,28},{28,24},{1,5},{5... | collective-permute-start | bytes 1277960 | tf_op jit(solution)/shard_map/ppermute | solution.py:850

commit v2 on v1

--- a/solution.py
+++ b/solution.py
@@ -407,7 +407,7 @@
             state[1] = state[1] + jnp.sum(apart, axis=0)
             state[2] = state[2] + jnp.sum(apart * apart, axis=0)
 
-    for a, b in pieces(wide, 10):
+    for a, b in pieces(wide, 6):
         convolve(act_ref, pair_ref, False, rows + 2, a, b, take)
         mover.put(mid_ref.at[a:b], mid_far.at[a:b])
     pilot, total, square = state

time: 111 us -> 111 us (level)
  no operation moved by 1% of the time
where the time goes in v2:
time: 111 us
  Pallas kernels  48.4 us (44%)
  starting transfers between devices  32.2 us (29%)
  blocking collectives  19.3 us (17%)
  waiting for transfers between devices  8.86 us (8%)
  between operations  1.2 us (1%)
    pallas_call x15, Pallas kernels, kernel_call(): pl.pallas_call(run, out_shape=(*(pltpu.HBM(out.shape, out.dtype) for out...  48.4 us
    all_to_all x1, blocking collectives, to_chips(): return lax.all_to_all(payload, AXES, 0, 0, axis_index_groups=groups)  19.3 us
    all_to_all x3, starting transfers between devices, to_all(): return lax.all_to_all(payload, AXES, 0, 0)  14.9 us
    all_to_all x3, waiting for transfers between devices, to_all(): return lax.all_to_all(payload, AXES, 0, 0)  6.61 us
    ppermute x4, starting transfers between devices, pair_exchange(): return (one, lax.ppermute(other, axis, pairs))  5.08 us
    ppermute x4, starting transfers between devices, pair_exchange(): one = lax.ppermute(one, axis, [(i, i ^ 1) for i in range(count)])  4.79 us
    ppermute x5, starting transfers between devices, to_sibling(): lax.ppermute(payload, 'ha', [(i, i ^ 1) for i in range(lax.axis_size('ha'...  3.87 us
    all_to_all x1, starting transfers between devices, to_chips(): return lax.all_to_all(payload, AXES, 0, 0, axis_index_groups=groups)  3.54 us
  transfers between devices with their start and end apart: 17, of which 5 were waited for; matrix products, arithmetic and copies ran while one was open for 1% of the time, Pallas kernels for 34%

profile of v2, /device:TPU:1, one launch (start us, length us, event | category | flops | bytes accessed | tf_op | source)
XLA Modules:
  0.0 110.7 jit_solution(16639498219512551193)
XLA Ops:
  0.6 2.7 %prepare_x.1 = (bf16[32,8,16,128]{3,2,1,0:T(8,128)(2,1)}, bf16[32,2,16,128]{3,2,1,0:T(8,128)(2,1)S(1)}, bf16[32,2,16,128]{3,2,1,0:T(8,128)(2,1)S(1)}, bf16[4,8,16,128]{3,2,1,0:T(8,128)(2,1)S(1)}, f32[8,128]{1,0:T(8,128)S(1)}) custom-call(bf16[16,8,32,128]{3,2,1,0:T(8,128)(2,1)} %refs_0_.3), custom_call_target="tpu_custom_call" | custom-call | flops 2529999872 | tf_op jit(solution)/shard_map/prepare_x/pallas_call | solution.py:57
  3.5 2.6 %collective-permute-start.1 = (bf16[32,2,16,128]{3,2,1,0:T(8,128)(2,1)S(1)}, bf16[32,2,16,128]{3,2,1,0:T(8,128)(2,1)S(1)}, u32[]{:S(2)}, u32[]{:S(2)}) collective-permute-start(bf16[32,2,16,128]{3,2,1,0:T(8,128)(2,1)S(1)} %get-tuple-element.65), channel_id=1, source_target_pairs={{0,28},{4,8},{8,4},{12,16},{16,12},{20,24},{24,20},{28,0},{1,29},{... | collective-permute-start | bytes 786440 | tf_op jit(solution)/shard_map/ppermute | solution.py:859
  6.1 2.6 %prepare_g.1 = (bf16[32,8,16,128]{3,2,1,0:T(8,128)(2,1)}, f32[32,8,128]{2,1,0:T(8,128)}, bf16[32,2,16,128]{3,2,1,0:T(8,128)(2,1)S(1)}, bf16[32,2,16,128]{3,2,1,0...) custom-call(bf16[16,8,32,128]{3,2,1,0:T(8,128)(2,1)} %refs_3_.1, ...), custom_call_target="tpu_custom_call" | custom-call | flops 2200000000 | tf_op jit(solution)/shard_map/prepare_g/pallas_call | solution.py:57
  8.7 5.1 %all-to-all-start = ((f32[32,8,128]{2,1,0:T(8,128)}), f32[32,8,128]{2,1,0:T(8,128)S(1)}, u32[]{:S(2)}, u32[]{:S(2)}) async-start(f32[32,8,128]{2,1,0:T(8,128)} %get-tuple-element.70), calls=%async_computation | async-start | bytes 262144 | tf_op jit(solution)/shard_map/all_to_all | solution.py:840
  13.9 1.5 %collective-permute-start.2 = (bf16[2,12,16,128]{3,2,1,0:T(8,128)(2,1)S(1)}, bf16[2,12,16,128]{3,2,1,0:T(8,128)(2,1)S(1)}, u32[]{:S(2)}, u32[]{:S(2)}) collective-permute-start(bf16[2,12,16,128]{3,2,1,0:T(8,128)(2,1)S(1)} %get-tuple-element.67), channel_id=1, source_target_pairs={{0,1},{1,0},{2,3},{3,2},{4,5},{5,4},{6,7},{7,6},{8,9},{9,8},{10,11... | collective-permute-start | bytes 294920 | tf_op jit(solution)/shard_map/ppermute | solution.py:858
  15.3 0.7 collective-permute-start.3
  16.0 0.7 collective-permute-start.4
  16.7 1.1 %collective-permute-start.5 = (bf16[32,2,16,128]{3,2,1,0:T(8,128)(2,1)S(1)}, bf16[32,2,16,128]{3,2,1,0:T(8,128)(2,1)S(1)}, u32[]{:S(2)}, u32[]{:S(2)}) collective-permute-start(bf16[32,2,16,128]{3,2,1,0:T(8,128)(2,1)S(1)} %get-tuple-element.74), channel_id=1, source_target_pairs={{0,28},{4,8},{8,4},{12,16},{16,12},{20,24},{24,20},{28,0},{1,29},{... | collective-permute-start | bytes 786440 | tf_op jit(solution)/shard_map/ppermute | solution.py:859
  18.4 2.7 %all-to-all-done.refs_6_ = f32[32,8,128]{2,1,0:T(8,128)S(1)} async-done(((f32[32,8,128]{2,1,0:T(8,128)}), f32[32,8,128]{2,1,0:T(8,128)S(1)}, u32[]{:S(2)}, u32[]{:S(2)}) %all-to-all-start) | async-done | bytes 131104 | tf_op jit(solution)/shard_map/all_to_all | solution.py:840
  21.1 5.5 %first_half.1 = (bf16[36,12,16,128]{3,2,1,0:T(8,128)(2,1)}, f32[34,10,16,128]{3,2,1,0:T(8,128)}, f32[32,8,128]{2,1,0:T(8,128)}, f32[2,16,128]{2,1,0:T(8,128)}) custom-call(bf16[32,8,16,128]{3,2,1,0:T(8,128)(2,1)} %get-tuple-element.63.refs_0_.refs_1_.refs_2_, bf16[3,3,128,128]{3,2,1,0:T(8,128)(2,1)} %refs_2_.3, ...), custom_call_target="tpu_custom_call" | custom-call | flops 6049999872 | tf_op jit(solution)/shard_map/first_half/pallas_call | solution.py:57
  26.7 2.5 %collective-permute-start.6 = (bf16[2,12,16,128]{3,2,1,0:T(8,128)(2,1)S(1)}, bf16[2,12,16,128]{3,2,1,0:T(8,128)(2,1)S(1)}, u32[]{:S(2)}, u32[]{:S(2)}) collective-permute-start(bf16[2,12,16,128]{3,2,1,0:T(8,128)(2,1)S(1)} %get-tuple-element.77), channel_id=1, source_target_pairs={{0,1},{1,0},{2,3},{3,2},{4,5},{5,4},{6,7},{7,6},{8,9},{9,8},{10,11... | collective-permute-start | bytes 294920 | tf_op jit(solution)/shard_map/ppermute | solution.py:858
  29.2 0.7 collective-permute-start.7
  29.9 5.1 %all-to-all-start.1 = ((f32[32,8,128]{2,1,0:T(8,128)}), f32[32,8,128]{2,1,0:T(8,128)S(1)}, u32[]{:S(2)}, u32[]{:S(2)}) async-start(f32[32,8,128]{2,1,0:T(8,128)} %get-tuple-element.80), calls=%async_computation.1 | async-start | bytes 262144 | tf_op jit(solution)/shard_map/all_to_all | solution.py:840
  35.0 6.1 %back_two.1 = (f32[34,10,16,128]{3,2,1,0:T(8,128)}, f32[16,256]{1,0:T(8,128)}, bf16[16,512]{1,0:T(8,128)(2,1)}) custom-call(bf16[32,8,16,128]{3,2,1,0:T(8,128)(2,1)} %get-tuple-element.72.refs_0_.refs_1_, bf16[3,3,128,128]{3,2,1,0:T(8,128)(2,1)} %refs_1_.5, bf16[4608,256]{1,0:T(8,128)(2,1)} %refs_0_.5, ...), custom_call_target="tpu_custom_call" | custom-call | flops 5500000256 | tf_op jit(solution)/shard_map/back_two/pallas_call | solution.py:57
  41.2 1.1 %all-to-all-done.1.refs_2_ = f32[32,8,128]{2,1,0:T(8,128)S(1)} async-done(((f32[32,8,128]{2,1,0:T(8,128)}), f32[32,8,128]{2,1,0:T(8,128)S(1)}, u32[]{:S(2)}, u32[]{:S(2)}) %all-to-all-start.1) | async-done | bytes 131104 | tf_op jit(solution)/shard_map/all_to_all | solution.py:840
  42.3 4.4 %second_norm.1 = (bf16[34,10,16,128]{3,2,1,0:T(8,128)(2,1)}, bf16[34,10,16,128]{3,2,1,0:T(8,128)(2,1)}, f32[32,8,128]{2,1,0:T(8,128)}, f32[2,16,128]{2,1,0:T(8,128)}, f32[2,16,128]{2,1,0:T(8,128)}) custom-call(f32[34,10,16,128]{3,2,1,0:T(8,128)} %get-tuple-element.71.refs_0_, f32[34,10,16,128]{3,2,1,0:T(8,128)} %get-tuple-element.79.refs_1_, ...), custom_call_target="tpu_custom_call" | custom-call | flops 3520000000 | tf_op jit(solution)/shard_map/second_norm/pallas_call | solution.py:57
  46.7 4.7 %all-to-all-start.2 = ((f32[32,8,128]{2,1,0:T(8,128)}), f32[32,8,128]{2,1,0:T(8,128)S(1)}, u32[]{:S(2)}, u32[]{:S(2)}) async-start(f32[32,8,128]{2,1,0:T(8,128)} %get-tuple-element.88), calls=%async_computation.2 | async-start | bytes 262144 | tf_op jit(solution)/shard_map/all_to_all | solution.py:840
  51.5 4.2 %kernel_two.1 = (f32[616,128]{1,0:T(8,128)}, f32[616,128]{1,0:T(8,128)}) custom-call(bf16[34,10,16,128]{3,2,1,0:T(8,128)(2,1)} %get-tuple-element.82.refs_0_, bf16[32,8,16,128]{3,2,1,0:T(8,128)(2,1)} %get-tuple-element.72.refs_0_.refs_1_, f32[2,16,128]{2,1,0:T(8,128)} %get-tuple-element.85.refs_2_, f32[16,128]{1,0:T(8,128)} %get-tuple-element.86.refs_3_.refs_6_), custom_call_target="tpu_custom_call" | custom-call | flops 3300000000 | tf_op jit(solution)/shard_map/kernel_two/pallas_call | solution.py:57
  56.0 2.8 %all-to-all-done.2.refs_4_ = f32[32,8,128]{2,1,0:T(8,128)S(1)} async-done(((f32[32,8,128]{2,1,0:T(8,128)}), f32[32,8,128]{2,1,0:T(8,128)S(1)}, u32[]{:S(2)}, u32[]{:S(2)}) %all-to-all-start.2) | async-done | bytes 131104 | tf_op jit(solution)/shard_map/all_to_all | solution.py:840
  58.8 5.0 %middle_grad.1 = (bf16[34,10,16,128]{3,2,1,0:T(8,128)(2,1)}, f32[584,128]{1,0:T(8,128)S(1)}, f32[584,128]{1,0:T(8,128)S(1)}, f32[616,128]{1,0:T(8,128)S(1)}, f32[16,128]{1,0:T(8,128)}) custom-call(f32[34,10,16,128]{3,2,1,0:T(8,128)} %get-tuple-element.71.refs_0_, bf16[34,10,16,128]{3,2,1,0:T(8,128)(2,1)} %get-tuple-element.83.refs_1_, ...), custom_call_target="tpu_custom_call" | custom-call | flops 6600000000 | tf_op jit(solution)/shard_map/middle_grad/pallas_call | solution.py:57
  63.8 1.4 %collective-permute-start.8 = (f32[584,128]{1,0:T(8,128)S(1)}, f32[584,128]{1,0:T(8,128)S(1)}, u32[]{:S(2)}, u32[]{:S(2)}) collective-permute-start(f32[584,128]{1,0:T(8,128)S(1)} %get-tuple-element.93), channel_id=1, source_target_pairs={{0,4},{4,0},{8,12},{12,8},{16,20},{20,16},{24,28},{28,24},{1,5},{5... | collective-permute-start | bytes 897032 | tf_op jit(solution)/shard_map/ppermute | solution.py:850
  65.2 1.2 %collective-permute-done.8.refs_1_ = f32[584,128]{1,0:T(8,128)S(1)} collective-permute-done((f32[584,128]{1,0:T(8,128)S(1)}, f32[584,128]{1,0:T(8,128)S(1)}, u32[]{:S(2)}, u32[]{:S(2)}) %collective-permute-start.8) | collective-permute-done | bytes 299040 | tf_op jit(solution)/shard_map/ppermute | solution.py:850
  66.4 1.1 pack_terms.1
  67.9 3.5 %all-to-all-start.3 = ((s16[16,80,128]{2,1,0:T(8,128)(2,1)}), s16[16,80,128]{2,1,0:T(8,128)(2,1)S(1)}, u32[]{:S(2)}, u32[]{:S(2)}) async-start(s16[16,80,128]{2,1,0:T(8,128)(2,1)} %get-tuple-element.99), calls=%async_computation.3 | async-start | bytes 655360 | tf_op jit(solution)/shard_map/all_to_all | solution.py:846
  71.5 5.6 %back_one.1 = (f32[32,8,16,128]{3,2,1,0:T(8,128)}, f32[16,128]{1,0:T(8,128)S(1)}) custom-call(bf16[34,10,16,128]{3,2,1,0:T(8,128)(2,1)} %get-tuple-element.90.refs_0_, bf16[32,8,16,128]{3,2,1,0:T(8,128)(2,1)} %get-tuple-element.63.refs_0_.refs_1_.refs_2_, bf16[3,3,128,128]{3,2,1,0:T(8,128)(2,1)} %refs_2_.3, f32[2,16,128]{2,1,0:T(8,128)} %get-tuple-element.76.refs_3_.refs_5_, ...), custom_call_target="tpu_custom_call" | custom-call | flops 5500000256 | tf_op jit(solution)/shard_map/back_one/pallas_call | solution.py:57
  77.3 4.7 %mix.1.refs_3_ = bf16[16,8,32,128]{3,2,1,0:T(8,128)(2,1)} custom-call(bf16[34,10,16,128]{3,2,1,0:T(8,128)(2,1)} %get-tuple-element.82.refs_0_, bf16[3,3,128,128]{3,2,1,0:T(8,128)(2,1)} %refs_1_.5, bf16[32,8,16,128]{3,2,1,0:T(8,128)(2,1)} %get-tuple-element.63.refs_0_.refs_1_.refs_2_, bf16[1,128]{1,0:T(2,128)(2,1)} %bitcast.26, ...), custom_call_target="tpu_custom_call" | custom-call | flops 3960000000 | tf_op jit(solution)/shard_map/mix/pallas_call | solution.py:57
  82.1 1.0 all-to-all-done.3.refs_0_
  83.1 1.0 add_terms.1
  84.1 19.3 %all_to_all.25.refs_4_.refs_0_ = bf16[16,104,128]{2,1,0:T(8,128)(2,1)S(1)} all-to-all(bf16[16,104,128]{2,1,0:T(8,128)(2,1)} %add_terms.1), channel_id=1, replica_groups={{0,1,2,3,8,9,10,11,16,17,18,19,24,25,26,27},{4,5,6,7,12,13,14,15,20,21,..., dimensions={0} | all-to-all | bytes 851968 | tf_op jit(solution)/shard_map/all_to_all | solution.py:846
  103.4 1.5 %collective-permute-start.12 = (bf16[16,104,128]{2,1,0:T(8,128)(2,1)S(1)}, bf16[16,104,128]{2,1,0:T(8,128)(2,1)S(1)}, u32[]{:S(2)}, u32[]{:S(2)}) collective-permute-start(bf16[16,104,128]{2,1,0:T(8,128)(2,1)S(1)} %all_to_all.25.refs_4_.refs_0_), channel_id=1, source_target_pairs={{0,4},{4,0},{8,12},{12,8},{16,20},{20,16},{24,28},{28,24},{1,5},{5... | collective-permute-start | bytes 1277960 | tf_op jit(solution)/shard_map/ppermute | solution.py:850
  104.9 4.4 %last_grads.1 = (bf16[16,8,32,128]{3,2,1,0:T(8,128)(2,1)}, f32[4608,256]{1,0:T(8,128)}, f32[16,4096]{1,0:T(8,128)}, f32[1,256]{1,0:T(1,128)}, f32[1,128]{1,0:T(1...) custom-call(bf16[4608,256]{1,0:T(8,128)(2,1)} %refs_0_.5, ...), custom_call_target="tpu_custom_call" | custom-call | flops 6600000000 | tf_op jit(solution)/shard_map/last_grads/pallas_call | solution.py:57
  109.4 1.1 %spread_out.1 = (f32[9,128,128]{2,1,0:T(8,128)}, f32[9,128,128]{2,1,0:T(8,128)}) custom-call(bf16[16,104,128]{2,1,0:T(8,128)(2,1)S(1)} %all_to_all.25.refs_4_.refs_0_, bf16[16,104,128]{2,1,0:T(8,128)(2,1)S(1)} %collective-permute-done.12.refs_1_, bf16[16,8,32,128]{3,2,1,0:T(8,128)(2,1)} %get-tuple-element.51.refs_2_), custom_call_target="tpu_custom_call" | custom-call | flops 2200000000 | tf_op jit(solution)/shard_map/spread_out/pallas_call | solution.py:57
  (45 shorter events, 1.9 us)
Async XLA Ops:
  3.4 10.4 %collective-permute-start = (bf16[32,2,16,128]{3,2,1,0:T(8,128)(2,1)S(1)}, bf16[32,2,16,128]{3,2,1,0:T(8,128)(2,1)S(1)}, u32[]{:S(2)}, u32[]{:S(2)}) collective-permute-start(bf16[32,2,16,128]{3,2,1,0:T(8,128)(2,1)S(1)} %get-tuple-element.64), channel_id=1, source_target_pairs={{0,4},{4,0},{8,12},{12,8},{16,20},{20,16},{24,28},{28,24},{1,5},{5... | collective-permute-start | bytes 786440 | tf_op jit(solution)/shard_map/ppermute | solution.py:858
  3.5 10.3 %collective-permute-start.1 = (bf16[32,2,16,128]{3,2,1,0:T(8,128)(2,1)S(1)}, bf16[32,2,16,128]{3,2,1,0:T(8,128)(2,1)S(1)}, u32[]{:S(2)}, u32[]{:S(2)}) collective-permute-start(bf16[32,2,16,128]{3,2,1,0:T(8,128)(2,1)S(1)} %get-tuple-element.65), channel_id=1, source_target_pairs={{0,28},{4,8},{8,4},{12,16},{16,12},{20,24},{24,20},{28,0},{1,29},{... | collective-permute-start | bytes 786440 | tf_op jit(solution)/shard_map/ppermute | solution.py:859
  6.1 11.7 %copy-start.12 = (bf16[256]{0:T(256)(128)(2,1)S(1)}, bf16[256]{0:T(256)(128)(2,1)}, u32[]{:S(2)}) copy-start(bf16[256]{0:T(256)(128)(2,1)} %param.27) | copy-start | bytes 1540
  8.7 12.4 %all-to-all-start = ((f32[32,8,128]{2,1,0:T(8,128)}), f32[32,8,128]{2,1,0:T(8,128)S(1)}, u32[]{:S(2)}, u32[]{:S(2)}) async-start(f32[32,8,128]{2,1,0:T(8,128)} %get-tuple-element.70), calls=%async_computation | async-start | bytes 262144 | tf_op jit(solution)/shard_map/all_to_all | solution.py:840
  13.9 7.2 %collective-permute-start.2 = (bf16[2,12,16,128]{3,2,1,0:T(8,128)(2,1)S(1)}, bf16[2,12,16,128]{3,2,1,0:T(8,128)(2,1)S(1)}, u32[]{:S(2)}, u32[]{:S(2)}) collective-permute-start(bf16[2,12,16,128]{3,2,1,0:T(8,128)(2,1)S(1)} %get-tuple-element.67), channel_id=1, source_target_pairs={{0,1},{1,0},{2,3},{3,2},{4,5},{5,4},{6,7},{7,6},{8,9},{9,8},{10,11... | collective-permute-start | bytes 294920 | tf_op jit(solution)/shard_map/ppermute | solution.py:858
  15.3 5.8 %collective-permute-start.3 = (bf16[2,12,16,128]{3,2,1,0:T(8,128)(2,1)S(1)}, bf16[2,12,16,128]{3,2,1,0:T(8,128)(2,1)S(1)}, u32[]{:S(2)}, u32[]{:S(2)}) collective-permute-start(bf16[2,12,16,128]{3,2,1,0:T(8,128)(2,1)S(1)} %get-tuple-element.68), channel_id=1, source_target_pairs={{0,0},{1,2},{2,1},{3,3},{4,4},{5,6},{6,5},{7,7},{8,8},{9,10},{10,9... | collective-permute-start | bytes 294920 | tf_op jit(solution)/shard_map/ppermute | solution.py:859
  16.0 10.6 %collective-permute-start.4 = (bf16[32,2,16,128]{3,2,1,0:T(8,128)(2,1)S(1)}, bf16[32,2,16,128]{3,2,1,0:T(8,128)(2,1)S(1)}, u32[]{:S(2)}, u32[]{:S(2)}) collective-permute-start(bf16[32,2,16,128]{3,2,1,0:T(8,128)(2,1)S(1)} %get-tuple-element.73), channel_id=1, source_target_pairs={{0,4},{4,0},{8,12},{12,8},{16,20},{20,16},{24,28},{28,24},{1,5},{5... | collective-permute-start | bytes 786440 | tf_op jit(solution)/shard_map/ppermute | solution.py:858
  16.7 9.9 %collective-permute-start.5 = (bf16[32,2,16,128]{3,2,1,0:T(8,128)(2,1)S(1)}, bf16[32,2,16,128]{3,2,1,0:T(8,128)(2,1)S(1)}, u32[]{:S(2)}, u32[]{:S(2)}) collective-permute-start(bf16[32,2,16,128]{3,2,1,0:T(8,128)(2,1)S(1)} %get-tuple-element.74), channel_id=1, source_target_pairs={{0,28},{4,8},{8,4},{12,16},{16,12},{20,24},{24,20},{28,0},{1,29},{... | collective-permute-start | bytes 786440 | tf_op jit(solution)/shard_map/ppermute | solution.py:859
  21.1 13.9 %copy-start.2 = (s32[16]{0:T(128)S(1)}, s32[16]{0:T(128)}, u32[]{:S(2)}) copy-start(s32[16]{0:T(128)} %refs_10_.1) | copy-start | bytes 196
  21.1 13.9 %copy-start.3 = (s32[16]{0:T(128)S(1)}, s32[16]{0:T(128)}, u32[]{:S(2)}) copy-start(s32[16]{0:T(128)} %refs_11_.2) | copy-start | bytes 196
  26.7 8.3 %collective-permute-start.6 = (bf16[2,12,16,128]{3,2,1,0:T(8,128)(2,1)S(1)}, bf16[2,12,16,128]{3,2,1,0:T(8,128)(2,1)S(1)}, u32[]{:S(2)}, u32[]{:S(2)}) collective-permute-start(bf16[2,12,16,128]{3,2,1,0:T(8,128)(2,1)S(1)} %get-tuple-element.77), channel_id=1, source_target_pairs={{0,1},{1,0},{2,3},{3,2},{4,5},{5,4},{6,7},{7,6},{8,9},{9,8},{10,11... | collective-permute-start | bytes 294920 | tf_op jit(solution)/shard_map/ppermute | solution.py:858
  29.2 5.8 %collective-permute-start.7 = (bf16[2,12,16,128]{3,2,1,0:T(8,128)(2,1)S(1)}, bf16[2,12,16,128]{3,2,1,0:T(8,128)(2,1)S(1)}, u32[]{:S(2)}, u32[]{:S(2)}) collective-permute-start(bf16[2,12,16,128]{3,2,1,0:T(8,128)(2,1)S(1)} %get-tuple-element.78), channel_id=1, source_target_pairs={{0,0},{1,2},{2,1},{3,3},{4,4},{5,6},{6,5},{7,7},{8,8},{9,10},{10,9... | collective-permute-start | bytes 294920 | tf_op jit(solution)/shard_map/ppermute | solution.py:859
  29.9 12.4 %all-to-all-start.1 = ((f32[32,8,128]{2,1,0:T(8,128)}), f32[32,8,128]{2,1,0:T(8,128)S(1)}, u32[]{:S(2)}, u32[]{:S(2)}) async-start(f32[32,8,128]{2,1,0:T(8,128)} %get-tuple-element.80), calls=%async_computation.1 | async-start | bytes 262144 | tf_op jit(solution)/shard_map/all_to_all | solution.py:840
  46.7 12.1 %all-to-all-start.2 = ((f32[32,8,128]{2,1,0:T(8,128)}), f32[32,8,128]{2,1,0:T(8,128)S(1)}, u32[]{:S(2)}, u32[]{:S(2)}) async-start(f32[32,8,128]{2,1,0:T(8,128)} %get-tuple-element.88), calls=%async_computation.2 | async-start | bytes 262144 | tf_op jit(solution)/shard_map/all_to_all | solution.py:840
  55.7 9.5 %collective-permute-start.9 = (f32[616,128]{1,0:T(8,128)}, f32[616,128]{1,0:T(8,128)S(1)}, u32[]{:S(2)}, u32[]{:S(2)}) collective-permute-start(f32[616,128]{1,0:T(8,128)} %get-tuple-element.95), channel_id=1, source_target_pairs={{0,4},{4,0},{8,12},{12,8},{16,20},{20,16},{24,28},{28,24},{1,5},{5... | collective-permute-start | bytes 946184 | tf_op jit(solution)/shard_map/ppermute | solution.py:850
  63.8 2.6 %collective-permute-start.8 = (f32[584,128]{1,0:T(8,128)S(1)}, f32[584,128]{1,0:T(8,128)S(1)}, u32[]{:S(2)}, u32[]{:S(2)}) collective-permute-start(f32[584,128]{1,0:T(8,128)S(1)} %get-tuple-element.93), channel_id=1, source_target_pairs={{0,4},{4,0},{8,12},{12,8},{16,20},{20,16},{24,28},{28,24},{1,5},{5... | collective-permute-start | bytes 897032 | tf_op jit(solution)/shard_map/ppermute | solution.py:850
  67.5 4.0 %collective-permute-start.10 = (f32[8,128]{1,0:T(8,128)S(1)}, f32[8,128]{1,0:T(8,128)S(1)}, u32[]{:S(2)}, u32[]{:S(2)}) collective-permute-start(f32[8,128]{1,0:T(8,128)S(1)} %get-tuple-element.96), channel_id=1, source_target_pairs={{0,4},{4,0},{8,12},{12,8},{16,20},{20,16},{24,28},{28,24},{1,5},{5... | collective-permute-start | bytes 12296 | tf_op jit(solution)/shard_map/ppermute | solution.py:850
  67.9 15.2 %all-to-all-start.3 = ((s16[16,80,128]{2,1,0:T(8,128)(2,1)}), s16[16,80,128]{2,1,0:T(8,128)(2,1)S(1)}, u32[]{:S(2)}, u32[]{:S(2)}) async-start(s16[16,80,128]{2,1,0:T(8,128)(2,1)} %get-tuple-element.99), calls=%async_computation.3 | async-start | bytes 655360 | tf_op jit(solution)/shard_map/all_to_all | solution.py:846
  77.0 5.0 %collective-permute-start.11 = (f32[16,128]{1,0:T(8,128)S(1)}, f32[16,128]{1,0:T(8,128)S(1)}, u32[]{:S(2)}, u32[]{:S(2)}) collective-permute-start(f32[16,128]{1,0:T(8,128)S(1)} %get-tuple-element.97.refs_4_.refs_1_), channel_id=1, source_target_pairs={{0,4},{4,0},{8,12},{12,8},{16,20},{20,16},{24,28},{28,24},{1,5},{5... | collective-permute-start | bytes 24584 | tf_op jit(solution)/shard_map/ppermute | solution.py:850
  82.0 22.9 %copy-start = (bf16[16,8,32,128]{3,2,1,0:T(8,128)(2,1)S(1)}, bf16[16,8,32,128]{3,2,1,0:T(8,128)(2,1)}, u32[]{:S(2)}) copy-start(bf16[16,8,32,128]{3,2,1,0:T(8,128)(2,1)} %refs_3_.1) | copy-start | bytes 3145732
  82.0 22.9 %copy-start.1 = (bf16[16,4096]{1,0:T(8,128)(2,1)S(1)}, bf16[16,4096]{1,0:T(8,128)(2,1)}, u32[]{:S(2)}) copy-start(bf16[16,4096]{1,0:T(8,128)(2,1)} %refs_11_.3) | copy-start | bytes 393220
  82.0 22.9 %copy-start.4 = (bf16[128]{0:T(256)(128)(2,1)S(1)}, bf16[128]{0:T(256)(128)(2,1)}, u32[]{:S(2)}) copy-start(bf16[128]{0:T(256)(128)(2,1)} %param.20) | copy-start | bytes 772
  82.0 22.9 %copy-start.5 = (bf16[128]{0:T(256)(128)(2,1)S(1)}, bf16[128]{0:T(256)(128)(2,1)}, u32[]{:S(2)}) copy-start(bf16[128]{0:T(256)(128)(2,1)} %param.24) | copy-start | bytes 772
  82.0 22.9 %copy-start.6 = (bf16[128]{0:T(256)(128)(2,1)S(1)}, bf16[128]{0:T(256)(128)(2,1)}, u32[]{:S(2)}) copy-start(bf16[128]{0:T(256)(128)(2,1)} %param.25) | copy-start | bytes 772
  82.0 22.9 %copy-start.7 = (f32[2,16,128]{2,1,0:T(8,128)S(1)}, f32[2,16,128]{2,1,0:T(8,128)}, u32[]{:S(2)}) copy-start(f32[2,16,128]{2,1,0:T(8,128)} %get-tuple-element.76.refs_3_.refs_5_) | copy-start | bytes 49156
  82.0 22.9 %copy-start.8 = (bf16[32,8,16,128]{3,2,1,0:T(8,128)(2,1)S(1)}, bf16[32,8,16,128]{3,2,1,0:T(8,128)(2,1)}, u32[]{:S(2)}) copy-start(bf16[32,8,16,128]{3,2,1,0:T(8,128)(2,1)} %get-tuple-element.63.refs_0_.refs_1_.refs_2_) | copy-start | bytes 3145732
  82.1 22.8 %copy-start.10 = (f32[16,256]{1,0:T(8,128)S(1)}, f32[16,256]{1,0:T(8,128)}, u32[]{:S(2)}) copy-start(f32[16,256]{1,0:T(8,128)} %get-tuple-element.81.refs_5_.refs_7_.refs_9_) | copy-start | bytes 49156
  82.1 22.8 %copy-start.11 = (bf16[16,512]{1,0:T(8,128)(2,1)S(1)}, bf16[16,512]{1,0:T(8,128)(2,1)}, u32[]{:S(2)}) copy-start(bf16[16,512]{1,0:T(8,128)(2,1)} %get-tuple-element.100.refs_10_) | copy-start | bytes 49156
  83.1 21.8 %copy-start.9 = (f32[32,8,16,128]{3,2,1,0:T(8,128)S(1)}, f32[32,8,16,128]{3,2,1,0:T(8,128)}, u32[]{:S(2)}) copy-start(f32[32,8,16,128]{3,2,1,0:T(8,128)} %get-tuple-element.98.refs_1_) | copy-start | bytes 6291460
  103.4 6.0 %collective-permute-start.12 = (bf16[16,104,128]{2,1,0:T(8,128)(2,1)S(1)}, bf16[16,104,128]{2,1,0:T(8,128)(2,1)S(1)}, u32[]{:S(2)}, u32[]{:S(2)}) collective-permute-start(bf16[16,104,128]{2,1,0:T(8,128)(2,1)S(1)} %all_to_all.25.refs_4_.refs_0_), channel_id=1, source_target_pairs={{0,4},{4,0},{8,12},{12,8},{16,20},{20,16},{24,28},{28,24},{1,5},{5... | collective-permute-start | bytes 1277960 | tf_op jit(solution)/shard_map/ppermute | solution.py:850
